TPU v7x, 32 devices: a whole 2x2x4 slice. The times are simulated.
32 devices in a mesh: groups: 2 (over y), dp: 16 (over z, x, core).
Axes of the slice: x: 2, y: 2, z: 4, core: 2. Of those that a mesh axis runs over, the one named last changes fastest.
Arguments:
- node_rows: bfloat16 [16384, 8192], P(('groups', 'dp')), parts along dimension 0, may hold values from -6 to 6
- kept_counts: int32 [64], P(('groups', 'dp')), parts along dimension 0, may hold values from 8 to 256, as said below
- parents: int32 [64, 256], P(('groups', 'dp')), parts along dimension 0, may hold values from 0 to 254, as said below
- cache_len: int32 [64], P(('groups', 'dp')), parts along dimension 0, may hold values from 128 to 1024
- cache_kv: bfloat16 [64, 2, 1024, 128], P(('groups', 'dp')), parts along dimension 0, may hold values from -480 to 480
- norm_gain: float32 [8192], replicated, may hold values from 0.5 to 2
- w_qkv: bfloat16 [8192, 1280], P('dp'), may hold values from -0.0625 to 0.0625
- b_qkv: float32 [1280], replicated, may hold values from -3 to 3
Outputs:
- attended: bfloat16 [16384, 1024], P(('groups', 'dp')), parts along dimension 0
There are 2 independent parts, one for each index of `groups`. A program takes and returns all parts, laid end to end along the dimension named above; an argument that names none is the same for every part. Nothing has to cross between parts.
Inputs may be any that keep to these rules, and one draw needn't show every extreme that they name: The counts of one part add up to exactly 3072; on some device every request keeps 256 nodes. The kept nodes of request r are its first kept_counts[r] slots. parents[r, 0] = 0, and 0 <= parents[r, i] < i for i >= 1.
All inputs are finite; a program needn't handle non-finite values.
Results may differ from a plain program's by a relative error of at most 0.0045.
The roundings to bfloat16 on the way count: a program that leaves them out, or rounds other values in their place, can miss the bound.
Values may be sent and summed in bfloat16 or wider, within the bound.
No kernel may reach another device: no remote copies, remote signals or barrier semaphores. Data moves between devices by JAX's collectives and lax.ppermute only.
A program may use at most 128 MiB of HBM per device.

v0:
```python
import jax
import jax.numpy as jnp
from jax import lax
from jax.sharding import PartitionSpec as P

HEAD = 128
GROUP = 8


EPSILON = 1e-06
ROPE_BASE = 1000000.0


def normalize(row_block, norm_gain):
    values32 = row_block.astype(jnp.float32)
    mean_square = jnp.mean(values32 * values32, axis=-1, keepdims=True)
    return (values32 * lax.rsqrt(mean_square + EPSILON) * norm_gain).astype(jnp.bfloat16)


def ancestry(parent_row):
    max_nodes = parent_row.shape[0]
    positions = jnp.arange(max_nodes, dtype=jnp.int32)
    parent_link = (parent_row[:, None] == positions[None, :]) & (positions[:, None] >= 1)
    reached = (parent_link | (positions[:, None] == positions[None, :])).astype(jnp.bfloat16)
    for squaring in range((max_nodes - 1).bit_length()):
        reached = jnp.minimum(
            jnp.dot(reached, reached, preferred_element_type=jnp.float32), 1.0
        ).astype(jnp.bfloat16)
    return reached


def spin(vectors, cosine, sine_part):
    half_size = vectors.shape[-1] // 2
    lower_half = vectors[..., :half_size]
    upper_half = vectors[..., half_size:]
    return jnp.concatenate(
        [
            lower_half * cosine - upper_half * sine_part,
            upper_half * cosine + lower_half * sine_part,
        ],
        axis=-1,
    )


def attend(bundle):
    projected, parent_row, kept_count, length, cache_pair = bundle
    max_nodes = projected.shape[0]
    reached = ancestry(parent_row)
    depth_of = jnp.sum(reached.astype(jnp.float32), axis=1) - 1.0
    placed = length.astype(jnp.float32) + depth_of
    frequency = ROPE_BASE ** (-(jnp.arange(HEAD // 2, dtype=jnp.float32) * 2.0 / HEAD))
    angles = placed[:, None] * frequency[None, :]
    cosine = jnp.cos(angles)
    sine_part = jnp.sin(angles)
    query_width = GROUP * HEAD
    queries = projected[:, :query_width].astype(jnp.float32).reshape(max_nodes, GROUP, HEAD)
    queries = spin(queries, cosine[:, None, :], sine_part[:, None, :]).astype(jnp.bfloat16)
    node_keys = spin(
        projected[:, query_width : query_width + HEAD].astype(jnp.float32), cosine, sine_part
    ).astype(jnp.bfloat16)
    node_values = projected[:, query_width + HEAD :]
    scaling = HEAD ** (-0.5)
    past_scores = (
        jnp.einsum("ngh,ch->ngc", queries, cache_pair[0], preferred_element_type=jnp.float32)
        * scaling
    )
    visible = jnp.arange(cache_pair.shape[1], dtype=jnp.int32) < length
    past_scores = jnp.where(visible[None, None, :], past_scores, -jnp.inf)
    tree_scores = (
        jnp.einsum("ngh,mh->ngm", queries, node_keys, preferred_element_type=jnp.float32) * scaling
    )
    tree_scores = jnp.where(reached[:, None, :] > 0, tree_scores, -jnp.inf)
    row_top = jnp.maximum(jnp.max(past_scores, axis=-1), jnp.max(tree_scores, axis=-1))[..., None]
    past_weights = jnp.exp(past_scores - row_top)
    tree_weights = jnp.exp(tree_scores - row_top)
    denominator = jnp.sum(past_weights, axis=-1, keepdims=True) + jnp.sum(
        tree_weights, axis=-1, keepdims=True
    )
    past_weights = (past_weights / denominator).astype(jnp.bfloat16)
    tree_weights = (tree_weights / denominator).astype(jnp.bfloat16)
    blended = jnp.einsum(
        "ngc,ch->ngh", past_weights, cache_pair[1], preferred_element_type=jnp.float32
    )
    blended = blended + jnp.einsum(
        "ngm,mh->ngh", tree_weights, node_values, preferred_element_type=jnp.float32
    )
    living = jnp.arange(max_nodes, dtype=jnp.int32) < kept_count
    blended = jnp.where(living[:, None, None], blended, 0.0)
    return blended.reshape(max_nodes, query_width).astype(jnp.bfloat16)


def on_device(node_rows, kept_counts, parents, cache_len, cache_kv, norm_gain, w_qkv, b_qkv):
    local_rows, width_in = node_rows.shape
    requests, max_nodes = parents.shape
    normed = normalize(node_rows, norm_gain)
    summed = jnp.dot(
        normed, lax.all_gather(w_qkv, "dp", axis=0, tiled=True), preferred_element_type=jnp.float32
    )
    projected = (summed + b_qkv).astype(jnp.bfloat16)
    per_request = projected.reshape(requests, max_nodes, projected.shape[1])
    attended = lax.map(attend, (per_request, parents, kept_counts, cache_len, cache_kv))
    return attended.reshape(local_rows, GROUP * HEAD)


def solution(mesh):
    return jax.shard_map(
        on_device,
        mesh=mesh,
        in_specs=(
            P(("groups", "dp"), None),
            P(("groups", "dp")),
            P(("groups", "dp"), None),
            P(("groups", "dp")),
            P(("groups", "dp"), None, None, None),
            P(),
            P("dp", None),
            P(),
        ),
        out_specs=P(("groups", "dp"), None),
        check_vma=False,
    )
```

profile of v0, /device:TPU:0, one launch (start us, length us, event | category | flops | bytes accessed | tf_op | source)
XLA Modules:
  0.0 199.2 jit_solution(2706104720419716621)
XLA Ops:
  6.5 0.0 all-gather.2.cloned.1.call-start
  6.5 0.7 all-gather.2.cloned.1.call-update
  7.3 5.1 %fusion.44 = f32[512]{0:T(512)S(1)} fusion(bf16[512,8192]{1,0:T(8,128)(2,1)} %param.10), kind=kLoop, calls=%fused_computation.82 | loop fusion | flops 12582400 | bytes 8390656 | tf_op jit(solution)/shard_map/reduce_sum | solution.py:16
  12.4 0.0 copy-start.4
  12.4 0.0 copy-start.5
  12.4 108.1 %all-gather.2.cloned.1.call-done = bf16[8192,1280]{1,0:T(8,128)(2,1)} async-done(((bf16[512,1280]{1,0:T(8,128)(2,1)}), bf16[8192,1280]{1,0:T(8,128)(2,1)}) %all-gather.2.cloned.1.call-update) | async-done | bytes 20971536 | tf_op jit(solution)/shard_map/all_gather | solution.py:97
  120.5 0.0 copy-done.2
  120.5 0.0 copy-done.3
  120.5 17.7 %fusion.54 = bf16[512,1280]{1,0:T(8,128)(2,1)} fusion(bf16[8192,1280]{1,0:T(8,128)(2,1)} %all-gather.2.cloned.1.call-done, bf16[512,8192]{1,0:T(8,128)(2,1)} %param.10, f32[8192]{0:T(1024)S(1)} %copy-done.2, f32[512]{0:T(512)S(1)} %add_rsqrt_fusion, f32[1280]{0:T(1024)S(1)} %copy-done.3), kind=kOutput, calls=%fused_computation.89 | convolution fusion | flops 10755506176 | bytes 30710784 | tf_op jit(solution)/shard_map/dot_general | solution.py:96
  138.2 0.0 copy-done.1
  138.2 0.0 copy-done.4
  138.3 54.1 %while.12 = (s32[]{:T(128)}, bf16[2,256,1024]{2,1,0:T(8,128)(2,1)}, s32[2]{0:T(128)S(1)}, s32[2]{0:T(128)S(1)}, bf16[2,256,1280]{2,1,0:T(8,128)(2,1)}, /*index=5...) while((s32[]{:T(128)}, bf16[2,256,1024]{2,1,0:T(8,128)(2,1)}, ...), condition=%wide.region_7.8_spmd, body=%wide.region_1.7_spmd.sunk | while | flops 1648080768 | bytes 84294088 | solution.py:101
  138.5 0.8 fusion.90
  139.2 0.4 fusion.91
  139.7 0.4 fusion.92
  140.1 1.1 convert_reduce_fusion.2
  141.2 0.6 dynamic_slice.42
  142.5 1.1 dynamic-slice_bitcast_fusion.8
  143.7 1.2 subtract_convert_fusion.4
  144.9 0.1 slice_convert_fusion.4
  145.0 0.3 copy.33
  145.4 0.1 fusion.89
  145.5 0.3 copy.34
  145.8 0.3 copy.35
  146.2 0.3 subtract_convert_fusion.5
  146.5 0.9 broadcast_compare_fusion.2
  147.4 1.6 fusion.94
  149.0 0.6 iota_compare_fusion.10
  149.6 2.4 %fusion.93 = (f32[256,8]{0,1:T(8,128)S(1)}, f32[256,8,1024]{2,0,1:T(8,128)S(1)}) fusion(pred[1024]{0:T(1024)(128)(4,1)S(1)} %iota_compare_fusion.10, bf16[2,2,1024,128]{3,2,1,0:T(8,128)(2,1)} %get-tuple-element.221, s32[]{:T(128)} %get-tuple-element.205, bf16[256,8,64]{2,0,1:T(8,128)(2,1)S(1)} %get-tuple-element.186, ...), kind=kOutput, calls=%fused_computation.3.clone.1 | convolution fusion | flops 544208896 | bytes 9184768 | tf_op jit(solution)/shard_map/while/body/eval_jaxpr/ngh,ch->ngc/dot_general | solution.py:64
  152.1 0.4 fusion.96
  152.6 2.8 %copy-done = f32[256,8,1024]{2,0,1:T(8,128)} copy-done((f32[256,8,1024]{2,0,1:T(8,128)}, f32[256,8,1024]{2,0,1:T(8,128)S(1)}, u32[]{:S(2)}) %copy-start) | copy-done | bytes 8388632 | tf_op jit(solution)/shard_map/while
  155.3 2.0 %fusion.95 = f32[256,8]{0,1:T(8,128)S(1)} fusion(f32[256,8,1024]{2,0,1:T(8,128)S(1)} %get-tuple-element.188, f32[256,8]{0,1:T(8,128)S(1)} %max.11, pred[1024]{0:T(1024)(128)(4,1)S(1)} %iota_compare_fusion.10), kind=kLoop, calls=%fused_computation.4.clone.1 | loop fusion | flops 8386560 | bytes 8406016 | tf_op jit(solution)/shard_map/while/body/eval_jaxpr/reduce_sum | solution.py:76
  157.4 4.9 %fusion.97 = f32[256,8,128]{0,2,1:T(8,128)S(1)} fusion(f32[256,8,1024]{2,0,1:T(8,128)} %copy-done, f32[256,8]{0,1:T(8,128)S(1)} %add.105, f32[256,8]{0,1:T(8,128)S(1)} %max.11, pred[1024]{0:T(1024)(128)(4,1)S(1)} %iota_compare_fusion.10, bf16[2,2,1024,128]{3,2,1,0:T(8,128)(2,1)} %get-tuple-element.221, s32[]{:T(128)} %get-tuple-element.205, s32[]{:T(128)S(6)} %add.106), kind=kOutput, calls=%fused_computation.5.clone.1 | convolution fusion | flops 547356672 | bytes 9717252 | tf_op jit(solution)/shard_map/while/body/eval_jaxpr/ngc,ch->ngh/dot_general | solution.py:81
  162.3 0.7 dynamic_slice.43
  163.0 0.7 iota_compare_fusion.12
  163.7 0.7 fusion.98
  164.4 0.2 copy.36
  164.6 0.8 constant_dynamic-update-slice_fusion.2
  165.4 0.8 fusion.90
  166.2 0.4 fusion.91
  166.6 0.4 fusion.92
  167.1 1.1 convert_reduce_fusion.2
  168.2 0.6 dynamic_slice.42
  169.5 1.1 dynamic-slice_bitcast_fusion.8
  170.6 1.2 subtract_convert_fusion.4
  171.9 0.1 slice_convert_fusion.4
  172.0 0.3 copy.33
  172.3 0.1 fusion.89
  172.4 0.3 copy.34
  172.8 0.3 copy.35
  173.1 0.3 subtract_convert_fusion.5
  173.4 0.9 broadcast_compare_fusion.2
  174.4 1.6 fusion.94
  176.0 0.6 iota_compare_fusion.10
  176.6 2.4 %fusion.93 = (f32[256,8]{0,1:T(8,128)S(1)}, f32[256,8,1024]{2,0,1:T(8,128)S(1)}) fusion(pred[1024]{0:T(1024)(128)(4,1)S(1)} %iota_compare_fusion.10, bf16[2,2,1024,128]{3,2,1,0:T(8,128)(2,1)} %get-tuple-element.221, s32[]{:T(128)} %get-tuple-element.205, bf16[256,8,64]{2,0,1:T(8,128)(2,1)S(1)} %get-tuple-element.186, ...), kind=kOutput, calls=%fused_computation.3.clone.1 | convolution fusion | flops 544208896 | bytes 9184768 | tf_op jit(solution)/shard_map/while/body/eval_jaxpr/ngh,ch->ngc/dot_general | solution.py:64
  179.1 0.4 fusion.96
  179.5 2.8 %copy-done = f32[256,8,1024]{2,0,1:T(8,128)} copy-done((f32[256,8,1024]{2,0,1:T(8,128)}, f32[256,8,1024]{2,0,1:T(8,128)S(1)}, u32[]{:S(2)}) %copy-start) | copy-done | bytes 8388632 | tf_op jit(solution)/shard_map/while
  182.3 2.0 %fusion.95 = f32[256,8]{0,1:T(8,128)S(1)} fusion(f32[256,8,1024]{2,0,1:T(8,128)S(1)} %get-tuple-element.188, f32[256,8]{0,1:T(8,128)S(1)} %max.11, pred[1024]{0:T(1024)(128)(4,1)S(1)} %iota_compare_fusion.10), kind=kLoop, calls=%fused_computation.4.clone.1 | loop fusion | flops 8386560 | bytes 8406016 | tf_op jit(solution)/shard_map/while/body/eval_jaxpr/reduce_sum | solution.py:76
  184.3 4.9 %fusion.97 = f32[256,8,128]{0,2,1:T(8,128)S(1)} fusion(f32[256,8,1024]{2,0,1:T(8,128)} %copy-done, f32[256,8]{0,1:T(8,128)S(1)} %add.105, f32[256,8]{0,1:T(8,128)S(1)} %max.11, pred[1024]{0:T(1024)(128)(4,1)S(1)} %iota_compare_fusion.10, bf16[2,2,1024,128]{3,2,1,0:T(8,128)(2,1)} %get-tuple-element.221, s32[]{:T(128)} %get-tuple-element.205, s32[]{:T(128)S(6)} %add.106), kind=kOutput, calls=%fused_computation.5.clone.1 | convolution fusion | flops 547356672 | bytes 9717252 | tf_op jit(solution)/shard_map/while/body/eval_jaxpr/ngc,ch->ngh/dot_general | solution.py:81
  189.2 0.7 dynamic_slice.43
  189.9 0.7 iota_compare_fusion.12
  190.6 0.7 fusion.98
  191.3 0.2 copy.36
  191.5 0.8 constant_dynamic-update-slice_fusion.2
  (22 shorter events, 0.1 us)
Async XLA Ops:
  6.5 114.0 %copy-start.2 = (f32[8192]{0:T(1024)S(1)}, f32[8192]{0:T(1024)}, u32[]{:S(2)}) copy-start(f32[8192]{0:T(1024)} %param.15) | copy-start | bytes 98308
  6.5 114.0 %copy-start.3 = (f32[1280]{0:T(1024)S(1)}, f32[1280]{0:T(1024)}, u32[]{:S(2)}) copy-start(f32[1280]{0:T(1024)} %param.17) | copy-start | bytes 15364
  6.5 114.0 %all-gather.2.cloned.1.call-start = ((), (), s32[]{:S(2)}) async-start(), calls=%async_computation | async-start | bytes 22282240 | tf_op jit(solution)/shard_map/all_gather | solution.py:97
  12.4 125.9 %copy-start.1 = (s32[2,256]{1,0:T(2,128)S(1)}, s32[2,256]{1,0:T(2,128)}, u32[]{:S(2)}) copy-start(s32[2,256]{1,0:T(2,128)} %param.12) | copy-start | bytes 6148
  12.4 125.9 %copy-start.4 = (s32[2]{0:T(128)S(1)}, s32[2]{0:T(128)}, u32[]{:S(2)}) copy-start(s32[2]{0:T(128)} %param.11) | copy-start | bytes 28
  12.4 125.9 %copy-start.5 = (s32[2]{0:T(128)S(1)}, s32[2]{0:T(128)}, u32[]{:S(2)}) copy-start(s32[2]{0:T(128)} %param.13) | copy-start | bytes 28
  152.1 3.2 %copy-start = (f32[256,8,1024]{2,0,1:T(8,128)}, f32[256,8,1024]{2,0,1:T(8,128)S(1)}, u32[]{:S(2)}) copy-start(f32[256,8,1024]{2,0,1:T(8,128)S(1)} %get-tuple-element.188) | copy-start | bytes 25165828 | tf_op jit(solution)/shard_map/while
  179.0 3.2 %copy-start = (f32[256,8,1024]{2,0,1:T(8,128)}, f32[256,8,1024]{2,0,1:T(8,128)S(1)}, u32[]{:S(2)}) copy-start(f32[256,8,1024]{2,0,1:T(8,128)S(1)} %get-tuple-element.188) | copy-start | bytes 25165828 | tf_op jit(solution)/shard_map/while
Sparse Core Ops, SparseCore 0:
  9.0 111.5 all-gather.1
where the time goes:
time: 200 us; the launch traced here: 199 us
  waiting for transfers between devices  109 us (54%)
  matrix products  42.5 us (21%)
  other arithmetic  18 us (9%)
  local copies, waits for them, and re-layouts  14.7 us (7%)
  between operations  13.4 us (7%)
    all_gather x1, waiting for transfers between devices, on_device(): lax.all_gather(w_qkv, 'dp', axis=0, tiled=True)  108 us
    dot_general x1, matrix products, on_device(): jnp.dot(normed, lax.all_gather(w_qkv, 'dp', axis=0, tiled=True), preferre...  17.7 us
    dot_general x2, matrix products, attend(): jnp.einsum('ngc,ch->ngh', past_weights, cache_pair[1], preferred_element_...  9.81 us
    while x8, local copies, waits for them, and re-layouts  6.84 us
    dot_general x8, matrix products, ancestry(): jnp.dot(reached, reached, preferred_element_type=jnp.float32)  5.48 us
    reduce_sum x1, other arithmetic, normalize(): mean_square = jnp.mean(values32 * values32, axis=-1, keepdims=True)  5.1 us
    dot_general x2, matrix products, attend(): jnp.einsum('ngh,ch->ngc', queries, cache_pair[0], preferred_element_type=...  4.9 us
    reduce_sum x2, other arithmetic, attend(): jnp.sum(past_weights, axis=-1, keepdims=True)  4.08 us
  transfers between devices with their start and end apart: 1, of which 1 were waited for; matrix products, arithmetic and copies ran while one was open for 3% of the time, Pallas kernels for 0%

commit v1 on v0

v1 whole, which is shorter than its diff:
```python
import functools
import math

import jax
import jax.numpy as jnp
from jax import lax
from jax.experimental import pallas as pl
from jax.experimental.pallas import tpu as pltpu
from jax.sharding import PartitionSpec as P

HEAD = 128
GROUP = 8
EPSILON = 1e-06
ROPE_BASE = 1000000.0
SCORE_SCALE = HEAD ** (-0.5) * math.log2(math.e)
HEADS_PER_STEP = 2


def normalize(row_block, norm_gain):
    values32 = row_block.astype(jnp.float32)
    mean_square = jnp.mean(values32 * values32, axis=-1, keepdims=True)
    return (values32 * lax.rsqrt(mean_square + EPSILON) * norm_gain).astype(jnp.bfloat16)


def tree_tables(parents, cache_len):
    max_nodes = parents.shape[1]
    positions = jnp.arange(max_nodes, dtype=jnp.int32)
    parent_link = (parents[:, :, None] == positions) & (positions[:, None] >= 1)
    reached = (parent_link | (positions[:, None] == positions)).astype(jnp.bfloat16)
    for squaring in range((max_nodes - 1).bit_length()):
        product = jnp.einsum("rij,rjk->rik", reached, reached, preferred_element_type=jnp.float32)
        reached = jnp.minimum(product, 1.0).astype(jnp.bfloat16)
    depth_of = jnp.sum(reached.astype(jnp.float32), axis=2) - 1.0
    placed = cache_len.astype(jnp.float32)[:, None] + depth_of
    frequency = ROPE_BASE ** (-(jnp.arange(HEAD // 2, dtype=jnp.float32) * 2.0 / HEAD))
    angles = placed[:, :, None] * frequency
    cosine = jnp.cos(angles)
    sine_part = jnp.sin(angles)
    tree_bias = jnp.where(reached > 0, 0.0, -jnp.inf).astype(jnp.float32)
    return (
        tree_bias,
        jnp.concatenate([cosine, cosine], axis=-1),
        jnp.concatenate([-sine_part, sine_part], axis=-1),
    )


def project_kernel(x_ref, w_ref, b_ref, o_ref, acc_ref):
    step = pl.program_id(0)
    part = jnp.dot(x_ref[...], w_ref[...], preferred_element_type=jnp.float32)

    @pl.when(step == 0)
    def _():
        acc_ref[...] = part

    @pl.when(step > 0)
    def _():
        acc_ref[...] += part

    @pl.when(step == pl.num_programs(0) - 1)
    def _():
        o_ref[...] = (acc_ref[...] + b_ref[...]).astype(o_ref.dtype)


def project(normed, weights, bias):
    rows, depth = normed.shape
    columns = weights.shape[1]
    tile = 1024
    return pl.pallas_call(
        project_kernel,
        out_shape=jax.ShapeDtypeStruct((rows, columns), jnp.bfloat16),
        grid=(depth // tile,),
        in_specs=[
            pl.BlockSpec((rows, tile), lambda k: (0, k)),
            pl.BlockSpec((tile, columns), lambda k: (k, 0)),
            pl.BlockSpec((1, columns), lambda k: (0, 0)),
        ],
        out_specs=pl.BlockSpec((rows, columns), lambda k: (0, 0)),
        scratch_shapes=[pltpu.VMEM((rows, columns), jnp.float32)],
        compiler_params=pltpu.CompilerParams(vmem_limit_bytes=48 * 2**20),
        cost_estimate=pl.CostEstimate(
            flops=2 * rows * depth * columns,
            bytes_accessed=2 * (rows * depth + depth * columns + rows * columns),
            transcendentals=0,
        ),
    )(normed, weights, bias.reshape(1, columns))


def rotate(vectors, cosine, sine_part):
    return (vectors * cosine + pltpu.roll(vectors, HEAD // 2, 1) * sine_part).astype(jnp.bfloat16)


def attend_kernel(kept_ref, len_ref, q_ref, kv_ref, bias_ref, cos_ref, sin_ref, cache_ref, o_ref, key_ref):
    request = pl.program_id(0)
    cosine = cos_ref[0]
    sine_part = sin_ref[0]

    @pl.when(pl.program_id(1) == 0)
    def _():
        key_ref[...] = rotate(kv_ref[:, :HEAD].astype(jnp.float32), cosine, sine_part)

    max_nodes = q_ref.shape[0]
    cache = cache_ref.shape[2]
    past = lax.broadcasted_iota(jnp.int32, (1, cache), 1) < len_ref[request]
    past_bias = jnp.where(past, 0.0, -jnp.inf)
    living = lax.broadcasted_iota(jnp.int32, (max_nodes, 1), 0) < kept_ref[request]
    transposed = (((1,), (1,)), ((), ()))
    for head in range(q_ref.shape[1] // HEAD):
        columns = slice(head * HEAD, (head + 1) * HEAD)
        query = rotate(q_ref[:, columns].astype(jnp.float32), cosine, sine_part)
        past_scores = lax.dot_general(query, cache_ref[0, 0], transposed, preferred_element_type=jnp.float32)
        past_scores = past_scores * SCORE_SCALE + past_bias
        tree_scores = lax.dot_general(query, key_ref[...], transposed, preferred_element_type=jnp.float32)
        tree_scores = tree_scores * SCORE_SCALE + bias_ref[0]
        top = jnp.maximum(
            jnp.max(past_scores, axis=1, keepdims=True), jnp.max(tree_scores, axis=1, keepdims=True)
        )
        past_weights = jnp.exp2(past_scores - top)
        tree_weights = jnp.exp2(tree_scores - top)
        total = jnp.sum(past_weights, axis=1, keepdims=True) + jnp.sum(tree_weights, axis=1, keepdims=True)
        inverse = 1.0 / total
        blended = jnp.dot(
            (past_weights * inverse).astype(jnp.bfloat16), cache_ref[0, 1], preferred_element_type=jnp.float32
        )
        blended += jnp.dot(
            (tree_weights * inverse).astype(jnp.bfloat16), kv_ref[:, HEAD:], preferred_element_type=jnp.float32
        )
        o_ref[:, columns] = jnp.where(living, blended, 0.0).astype(o_ref.dtype)


def attend(projected, tree_bias, cosine, sine_part, kept_counts, cache_len, cache_kv):
    requests, max_nodes = tree_bias.shape[:2]
    cache = cache_kv.shape[2]
    width = HEADS_PER_STEP * HEAD
    table = pl.BlockSpec((1, max_nodes, HEAD), lambda r, h, *_: (r, 0, 0))
    return pl.pallas_call(
        attend_kernel,
        out_shape=jax.ShapeDtypeStruct((requests * max_nodes, GROUP * HEAD), jnp.bfloat16),
        grid_spec=pltpu.PrefetchScalarGridSpec(
            num_scalar_prefetch=2,
            grid=(requests, GROUP // HEADS_PER_STEP),
            in_specs=[
                pl.BlockSpec((max_nodes, width), lambda r, h, *_: (r, h)),
                pl.BlockSpec((max_nodes, 2 * HEAD), lambda r, h, *_: (r, GROUP // 2)),
                pl.BlockSpec((1, max_nodes, max_nodes), lambda r, h, *_: (r, 0, 0)),
                table,
                table,
                pl.BlockSpec((1, 2, cache, HEAD), lambda r, h, *_: (r, 0, 0, 0)),
            ],
            out_specs=pl.BlockSpec((max_nodes, width), lambda r, h, *_: (r, h)),
            scratch_shapes=[pltpu.VMEM((max_nodes, HEAD), jnp.bfloat16)],
        ),
        compiler_params=pltpu.CompilerParams(vmem_limit_bytes=40 * 2**20),
    )(kept_counts, cache_len, projected, projected, tree_bias, cosine, sine_part, cache_kv)


def on_device(node_rows, kept_counts, parents, cache_len, cache_kv, norm_gain, w_qkv, b_qkv):
    weights = lax.all_gather(w_qkv, "dp", axis=0, tiled=True)
    normed = normalize(node_rows, norm_gain)
    tables = tree_tables(parents, cache_len)
    normed, weights, tables = lax.optimization_barrier((normed, weights, tables))
    projected = project(normed, weights, b_qkv)
    return attend(projected, *tables, kept_counts, cache_len, cache_kv)


def solution(mesh):
    return jax.shard_map(
        on_device,
        mesh=mesh,
        in_specs=(
            P(("groups", "dp"), None),
            P(("groups", "dp")),
            P(("groups", "dp"), None),
            P(("groups", "dp")),
            P(("groups", "dp"), None, None, None),
            P(),
            P("dp", None),
            P(),
        ),
        out_specs=P(("groups", "dp"), None),
        check_vma=False,
    )
```

time: 200 us -> 161 us (0.81)
  matrix products: 42.5 us -> 3.31 us
  Pallas kernels: 0 us -> 33.7 us
  waiting for transfers between devices: 109 us -> 92.8 us
  local copies, waits for them, and re-layouts: 14.7 us -> 0.72 us
    dot_general x17 -> x4, matrix products: 42.5 us -> 3.31 us  [tree_tables(): jnp.einsum('rij,rjk->rik', reached, reached, preferred_element_type=jnp.f...]
    pallas_call x0 -> x2, Pallas kernels: none -> 33.7 us  [the longest x1 17.5 us: project(): pl.pallas_call(project_kernel, out_shape=jax.ShapeDtypeStruct((rows, colu...]
    all_gather x1, waiting for transfers between devices: 108 us -> 92.1 us  [on_device(): weights = lax.all_gather(w_qkv, 'dp', axis=0, tiled=True)]
    convert_element_type x2, other arithmetic: 0.02 us -> 10.8 us  [the longest x1 10.1 us: normalize(): (values32 * lax.rsqrt(mean_square + EPSILON) * norm_gain).astype(jnp.bflo...]
    while x8 -> x0, local copies, waits for them, and re-layouts: 6.84 us -> none
    reduce_sum x4 -> x0, other arithmetic: 4.96 us -> none  [the longest x2 4.08 us: attend(): jnp.sum(past_weights, axis=-1, keepdims=True)]
    another operation x4 -> x0, other arithmetic: 3.07 us -> none
    dynamic_slice x6 -> x0, local copies, waits for them, and re-layouts: 2.64 us -> none  [on_device(): lax.map(attend, (per_request, parents, kept_counts, cache_len, cache_kv))]
  transfers between devices with their start and end apart: 1 -> 1, of which waited for: 1 -> 1; matrix products, arithmetic and copies ran while one was open for 3% -> 13% of each run, Pallas kernels for 0% -> 0%
where the time goes in v1:
time: 161 us
  waiting for transfers between devices  92.8 us (58%)
  Pallas kernels  33.7 us (21%)
  other arithmetic  17.2 us (11%)
  between operations  13.5 us (8%)
  matrix products  3.31 us (2%)
    all_gather x1, waiting for transfers between devices, on_device(): weights = lax.all_gather(w_qkv, 'dp', axis=0, tiled=True)  92.1 us
    pallas_call x1, Pallas kernels, project(): pl.pallas_call(project_kernel, out_shape=jax.ShapeDtypeStruct((rows, colu...  17.5 us
    pallas_call x1, Pallas kernels, attend(): pl.pallas_call(attend_kernel, out_shape=jax.ShapeDtypeStruct((requests *...  16.2 us
    convert_element_type x1, other arithmetic, normalize(): (values32 * lax.rsqrt(mean_square + EPSILON) * norm_gain).astype(jnp.bflo...  10.1 us
    reduce_sum x1, other arithmetic, normalize(): mean_square = jnp.mean(values32 * values32, axis=-1, keepdims=True)  5.1 us
    dot_general x4, matrix products, tree_tables(): jnp.einsum('rij,rjk->rik', reached, reached, preferred_element_type=jnp.f...  3.31 us
  transfers between devices with their start and end apart: 1, of which 1 were waited for; matrix products, arithmetic and copies ran while one was open for 13% of the time, Pallas kernels for 0%

profile of v1, /device:TPU:0, one launch (start us, length us, event | category | flops | bytes accessed | tf_op | source)
XLA Modules:
  0.0 161.1 jit_solution(6355215133051279027)
XLA Ops:
  6.5 0.0 copy-start.3
  6.5 0.0 all-gather.2.cloned.1.call-start
  6.5 0.7 all-gather.2.cloned.1.call-update
  7.3 0.7 convert_element_type.47
  7.9 0.7 reshape.56.b_ref
  8.7 1.7 %fusion.4 = bf16[2,256,256]{2,1,0:T(8,128)(2,1)S(1)} fusion(s32[2,256]{1,0:T(2,128)} %param.10, pred[256]{0:T(512)(128)(4,1)S(1)} %iota_compare_fusion.2, pred[256,256]{1,0:T(8,128)(4,1)S(1)} %iota_compare_fusion.1), kind=kOutput, calls=%fused_computation.14 | convolution fusion | flops 135135232 | bytes 329984 | tf_op jit(solution)/shard_map/rij,rjk->rik/dot_general | solution.py:31
  10.4 0.5 fusion.6
  10.9 0.5 fusion.8
  11.4 0.6 convert_reduce_fusion
  12.0 0.1 add_add_fusion
  12.1 1.0 fusion.25
  13.1 0.2 pad_maximum_fusion
  13.3 5.1 %fusion = f32[512]{0:T(512)S(1)} fusion(bf16[512,8192]{1,0:T(8,128)(2,1)} %param.8), kind=kLoop, calls=%fused_computation.2 | loop fusion | flops 12582400 | bytes 8390656 | tf_op jit(solution)/shard_map/reduce_sum | solution.py:21
  18.4 0.0 copy-done.3
  18.4 10.1 %fusion.2.x_ref = bf16[512,8192]{1,0:T(8,128)(2,1)} fusion(bf16[512,8192]{1,0:T(8,128)(2,1)} %param.8, f32[8192]{0:T(1024)S(1)} %copy-done.3, f32[512]{0:T(512)S(1)} %add_rsqrt_fusion), kind=kLoop, calls=%fused_computation.4 | loop fusion | flops 16777216 | bytes 16812032 | tf_op jit(solution)/shard_map/convert_element_type | solution.py:22
  28.5 92.1 %all-gather.2.cloned.1.call-done.w_ref = bf16[8192,1280]{1,0:T(8,128)(2,1)} async-done(((bf16[512,1280]{1,0:T(8,128)(2,1)}), bf16[8192,1280]{1,0:T(8,128)(2,1)}) %all-gather.2.cloned.1.call-update) | async-done | bytes 20971536 | tf_op jit(solution)/shard_map/all_gather | solution.py:157
  120.6 0.0 copy-start
  120.6 0.0 copy-start.1
  120.6 0.0 copy-start.2
  120.6 17.5 %shard_map.82.q_ref.kv_ref = bf16[512,1280]{1,0:T(8,128)(2,1)S(1)} custom-call(bf16[512,8192]{1,0:T(8,128)(2,1)} %fusion.2.x_ref, bf16[8192,1280]{1,0:T(8,128)(2,1)} %all-gather.2.cloned.1.call-done.w_ref, f32[1,1280]{1,0:T(1,128)S(1)} %reshape.56.b_ref), custom_call_target="tpu_custom_call" | custom-call | flops 10737418240 | bytes 30670848 | tf_op jit(solution)/shard_map/pallas_call | solution.py:68
  138.1 0.0 copy-done
  138.1 0.0 copy-done.1
  138.1 0.0 copy-done.2
  138.1 16.2 %shard_map.83 = bf16[512,1024]{1,0:T(8,128)(2,1)} custom-call(s32[2]{0:T(128)S(1)} %copy-done.1, s32[2]{0:T(128)S(1)} %copy-done.2, bf16[512,1280]{1,0:T(8,128)(2,1)S(1)} %shard_map.82.q_ref.kv_ref, bf16[512,1280]{1,0:T(8,128)(2,1)S(1)} %shard_map.82.q_ref.kv_ref, f32[2,256,256]{2,1,0:T(8,128)S(1)} %get-tuple-element.12.bias_ref, ...), custom_call_target="tpu_custom_call" | custom-call | tf_op jit(solution)/shard_map/pallas_call | solution.py:135
  (4 shorter events, 0.1 us)
Async XLA Ops:
  6.5 11.9 %copy-start.3 = (f32[8192]{0:T(1024)S(1)}, f32[8192]{0:T(1024)}, u32[]{:S(2)}) copy-start(f32[8192]{0:T(1024)} %param.13) | copy-start | bytes 98308
  6.5 114.0 %all-gather.2.cloned.1.call-start = ((), (), s32[]{:S(2)}) async-start(), calls=%async_computation | async-start | bytes 22282240 | tf_op jit(solution)/shard_map/all_gather | solution.py:157
  120.6 17.5 %copy-start = (bf16[2,2,1024,128]{3,2,1,0:T(8,128)(2,1)S(1)}, bf16[2,2,1024,128]{3,2,1,0:T(8,128)(2,1)}, u32[]{:S(2)}) copy-start(bf16[2,2,1024,128]{3,2,1,0:T(8,128)(2,1)} %cache_ref.1) | copy-start | bytes 3145732
  120.6 17.5 %copy-start.1 = (s32[2]{0:T(128)S(1)}, s32[2]{0:T(128)}, u32[]{:S(2)}) copy-start(s32[2]{0:T(128)} %kept_ref.1) | copy-start | bytes 28
  120.6 17.5 %copy-start.2 = (s32[2]{0:T(128)S(1)}, s32[2]{0:T(128)}, u32[]{:S(2)}) copy-start(s32[2]{0:T(128)} %len_ref.1) | copy-start | bytes 28
Sparse Core Ops, SparseCore 0:
  9.0 111.5 all-gather.1

commit v2 on v1

--- a/solution.py
+++ b/solution.py
@@ -76,7 +76,7 @@
         ],
         out_specs=pl.BlockSpec((rows, columns), lambda k: (0, 0)),
         scratch_shapes=[pltpu.VMEM((rows, columns), jnp.float32)],
-        compiler_params=pltpu.CompilerParams(vmem_limit_bytes=48 * 2**20),
+        compiler_params=pltpu.CompilerParams(vmem_limit_bytes=60 * 2**20),
         cost_estimate=pl.CostEstimate(
             flops=2 * rows * depth * columns,
             bytes_accessed=2 * (rows * depth + depth * columns + rows * columns),
@@ -149,11 +149,258 @@
             out_specs=pl.BlockSpec((max_nodes, width), lambda r, h, *_: (r, h)),
             scratch_shapes=[pltpu.VMEM((max_nodes, HEAD), jnp.bfloat16)],
         ),
-        compiler_params=pltpu.CompilerParams(vmem_limit_bytes=40 * 2**20),
+        compiler_params=pltpu.CompilerParams(vmem_limit_bytes=60 * 2**20),
     )(kept_counts, cache_len, projected, projected, tree_bias, cosine, sine_part, cache_kv)
 
 
+def norm_kernel(steps, core_ref, x_ref, other_ref, gain_ref, w_ref, *refs):
+    out_ref, copy_ref = refs[-2:]
+    copy_ref[...] = w_ref[...]
+
+    def work(rows_ref):
+        values32 = rows_ref[...].astype(jnp.float32)
+        mean_square = jnp.mean(values32 * values32, axis=-1, keepdims=True)
+        factor = lax.rsqrt(mean_square + EPSILON)
+        width = rows_ref.shape[1] // (2 * CHIPS)
+        for chip in range(CHIPS):
+            source = pl.ds(pl.multiple_of((2 * chip + core_ref[0]) * width, width), width)
+            block = rows_ref[:, source].astype(jnp.float32) * factor * gain_ref[:, source]
+            out_ref[:, chip * width : (chip + 1) * width] = block.astype(jnp.bfloat16)
+
+    pl.when(pl.program_id(0) < steps)(lambda: work(x_ref))
+    pl.when(pl.program_id(0) >= steps)(lambda: work(other_ref))
+
+
+def normalize_both(own_rows, other_rows, norm_gain, core, columns, unread):
+    rows, depth = own_rows.shape
+    tile = 128
+    steps = rows // tile
+    copy_spec = pl.BlockSpec((columns.shape[0] // (2 * steps), columns.shape[1]), lambda r, *_: (r, 0))
+    return pl.pallas_call(
+        functools.partial(norm_kernel, steps),
+        out_shape=(
+            jax.ShapeDtypeStruct((2 * rows, depth // 2), jnp.bfloat16),
+            jax.ShapeDtypeStruct(columns.shape, columns.dtype),
+        ),
+        grid_spec=pltpu.PrefetchScalarGridSpec(
+            num_scalar_prefetch=1,
+            grid=(2 * steps,),
+            in_specs=[
+                pl.BlockSpec((tile, depth), lambda r, *_: (jnp.minimum(r, steps - 1), 0)),
+                pl.BlockSpec((tile, depth), lambda r, *_: (jnp.maximum(r - steps, 0), 0)),
+                pl.BlockSpec((1, depth), lambda r, *_: (0, 0)),
+                copy_spec,
+                *[pl.BlockSpec(memory_space=pl.ANY)] * len(unread),
+            ],
+            out_specs=(pl.BlockSpec((tile, depth // 2), lambda r, *_: (r, 0)), copy_spec),
+        ),
+        compiler_params=pltpu.CompilerParams(vmem_limit_bytes=NORM_LIMIT * 2**20),
+        cost_estimate=pl.CostEstimate(flops=8 * rows * depth, bytes_accessed=6 * rows * depth, transcendentals=0),
+    )(core.reshape(1), own_rows, other_rows, norm_gain.reshape(1, depth), columns, *unread)
+
+
+def accumulate_kernel(count, unread, first, steps, copies, place_ref, *refs):
+    refs = refs[: 2 * count] + refs[2 * count + unread :]
+    if copies:
+        refs[-1][...] = refs[2 * count][...]
+        refs = refs[: 2 * count] + refs[2 * count + 1 : -1]
+    x_refs, piece_refs, rest = refs[:count], refs[count : 2 * count], refs[2 * count :]
+
+    def side(which):
+        total = None if first else rest[which][...]
+        for x_ref, w_ref in zip(x_refs, piece_refs):
+            part = jnp.dot(x_ref[...], w_ref[...], preferred_element_type=jnp.float32)
+            total = part if total is None else total + part
+        rest[which if first else 2 + which][...] = total
+
+    pl.when(pl.program_id(0) < steps)(lambda: side(1))
+    pl.when(pl.program_id(0) >= steps)(lambda: side(0))
+
+
+def accumulate(normed, pieces, sums, copied=None, unread=()):
+    rows = normed.shape[0] // 2
+    columns = pieces[0][0].shape[1]
+    tile = 256
+    steps = rows // tile
+    count = len(pieces)
+    depth = sum(array.shape[0] for array, _ in pieces)
+    places = jnp.stack([place for _, place in pieces]).astype(jnp.int32)
+
+    def rows_spec(index):
+        return pl.BlockSpec(
+            (tile, pieces[index][0].shape[0]), lambda r, place_ref: (lax.rem(r + steps, 2 * steps), place_ref[index])
+        )
+
+    sum_specs = (
+        pl.BlockSpec((tile, columns), lambda r, *_: (jnp.maximum(r - steps, 0), 0)),
+        pl.BlockSpec((tile, columns), lambda r, *_: (jnp.minimum(r, steps - 1), 0)),
+    )
+    out = jax.ShapeDtypeStruct((rows, columns), jnp.float32)
+    first = sums is None
+    extra = [] if copied is None else [copied]
+    copy_specs = [pl.BlockSpec((array.shape[0] // (2 * steps), array.shape[1]), lambda r, *_: (r, 0)) for array in extra]
+    return pl.pallas_call(
+        functools.partial(accumulate_kernel, count, len(unread), first, steps, bool(extra)),
+        out_shape=(out, out, *[jax.ShapeDtypeStruct(array.shape, array.dtype) for array in extra]),
+        grid_spec=pltpu.PrefetchScalarGridSpec(
+            num_scalar_prefetch=1,
+            grid=(2 * steps,),
+            in_specs=[rows_spec(i) for i in range(count)]
+            + [pl.BlockSpec(array.shape, lambda r, *_: (0, 0)) for array, _ in pieces]
+            + [pl.BlockSpec(memory_space=pl.ANY)] * len(unread)
+            + copy_specs
+            + ([] if first else list(sum_specs)),
+            out_specs=(*sum_specs, *copy_specs),
+        ),
+        input_output_aliases={} if first else {1 + 2 * count + len(unread) + len(extra) + i: i for i in range(2)},
+        compiler_params=pltpu.CompilerParams(vmem_limit_bytes=DOT_LIMIT * 2**20),
+        cost_estimate=pl.CostEstimate(
+            flops=4 * rows * depth * columns,
+            bytes_accessed=4 * rows * depth + 2 * depth * columns + (8 if first else 16) * rows * columns,
+            transcendentals=0,
+        ),
+    )(places, *([normed] * count), *[array for array, _ in pieces], *unread, *extra, *(() if first else sums))
+
+
+def softmax_values(query, past_keys, past_values, past_bias, node_keys, node_values, tree_bias, living):
+    transposed = (((1,), (1,)), ((), ()))
+    past_scores = lax.dot_general(query, past_keys, transposed, preferred_element_type=jnp.float32)
+    past_scores = past_scores * SCORE_SCALE + past_bias
+    tree_scores = lax.dot_general(query, node_keys, transposed, preferred_element_type=jnp.float32)
+    tree_scores = tree_scores * SCORE_SCALE + tree_bias
+    top = jnp.maximum(jnp.max(past_scores, axis=1, keepdims=True), jnp.max(tree_scores, axis=1, keepdims=True))
+    past_weights = jnp.exp2(past_scores - top)
+    tree_weights = jnp.exp2(tree_scores - top)
+    total = jnp.sum(past_weights, axis=1, keepdims=True) + jnp.sum(tree_weights, axis=1, keepdims=True)
+    inverse = 1.0 / total
+    blended = jnp.dot((past_weights * inverse).astype(jnp.bfloat16), past_values, preferred_element_type=jnp.float32)
+    blended += jnp.dot((tree_weights * inverse).astype(jnp.bfloat16), node_values, preferred_element_type=jnp.float32)
+    return jnp.where(living, blended, 0.0).astype(jnp.bfloat16)
+
+
+def masks(kept_ref, len_ref, request, max_nodes, cache):
+    past = lax.broadcasted_iota(jnp.int32, (1, cache), 1) < len_ref[request]
+    living = lax.broadcasted_iota(jnp.int32, (max_nodes, 1), 0) < kept_ref[request]
+    return jnp.where(past, 0.0, -jnp.inf), living
+
+
+def heads_kernel(kept_ref, len_ref, own_b, got_b, own_a, got_a, b_ref, bias_ref, cos_ref, sin_ref, cache_ref, o_ref):
+    past_bias, living = masks(kept_ref, len_ref, pl.program_id(0), own_a.shape[0], cache_ref.shape[2])
+    cosine, sine_part = cos_ref[0], sin_ref[0]
+
+    def column_block(index):
+        own_ref, got_ref, start = (own_b, got_b, 0) if index * HEAD < SPLIT else (own_a, got_a, SPLIT)
+        columns = slice(index * HEAD - start, (index + 1) * HEAD - start)
+        bias = b_ref[:, index * HEAD : (index + 1) * HEAD]
+        return (own_ref[:, columns] + got_ref[:, columns] + bias).astype(jnp.bfloat16)
+
+    node_keys = rotate(column_block(GROUP).astype(jnp.float32), cosine, sine_part)
+    node_values = column_block(GROUP + 1)
+    for head in reversed(range(GROUP)):
+        query = rotate(column_block(head).astype(jnp.float32), cosine, sine_part)
+        o_ref[:, head * HEAD : (head + 1) * HEAD] = softmax_values(
+            query, cache_ref[0, 0], cache_ref[0, 1], past_bias, node_keys, node_values, bias_ref[0], living
+        )
+
+
+def attend_sums(parts, bias, tables, kept_counts, cache_len, cache_kv):
+    requests, max_nodes = tables[0].shape[:2]
+    cache = cache_kv.shape[2]
+    rows = requests * max_nodes
+    scores = rows * GROUP * (cache + max_nodes)
+    table = pl.BlockSpec((1, max_nodes, HEAD), lambda r, *_: (r, 0, 0))
+    return pl.pallas_call(
+        heads_kernel,
+        out_shape=jax.ShapeDtypeStruct((rows, GROUP * HEAD), jnp.bfloat16),
+        grid_spec=pltpu.PrefetchScalarGridSpec(
+            num_scalar_prefetch=2,
+            grid=(requests,),
+            in_specs=[pl.BlockSpec((max_nodes, part.shape[1]), lambda r, *_: (r, 0)) for part in parts]
+            + [
+                pl.BlockSpec(bias.shape, lambda r, *_: (0, 0)),
+                pl.BlockSpec((1, max_nodes, max_nodes), lambda r, *_: (r, 0, 0)),
+                table,
+                table,
+                pl.BlockSpec((1, 2, cache, HEAD), lambda r, *_: (r, 0, 0, 0)),
+            ],
+            out_specs=pl.BlockSpec((max_nodes, GROUP * HEAD), lambda r, *_: (r, 0)),
+        ),
+        compiler_params=pltpu.CompilerParams(vmem_limit_bytes=HEADS_LIMIT * 2**20),
+        cost_estimate=pl.CostEstimate(flops=4 * scores * HEAD, bytes_accessed=4 * scores, transcendentals=scores),
+    )(kept_counts, cache_len, *parts, bias, *tables, cache_kv)
+
+
+Z = 4
+CHIPS = 2 * Z
+SPLIT = 3 * HEAD
+NORM_LIMIT = DOT_LIMIT = HEADS_LIMIT = 60
+
+GATE = ("a", ("own", "x0", "z1", "x1", "yx0", "yz1"))
+MIDDLE = ("a", ("z2", "z3", "x3", "yz3", "yx1"))
+LAST = ("a", ("yz2", "yx3", "x2", "yx2"))
+PLAN = (
+    "a + z0 z1", "a x z0 x0", "a x z1 x1", "a y z1 yz1", "a - w0 z3", "a + z1 z2", "a x z3 x3", "a y x0 yx0",
+    "b + z0 z1", "b x z0 x0", "a y z3 yz3", GATE, "b - w0 z3", "b x z1 x1", "a y x1 yx1", "b + z1 z2", "b x z3 x3",
+    "a y z2 yz2", "a x z2 x2", "a y x3 yx3", "b x z2 x2", "a y x2 yx2",
+    MIDDLE, LAST, ("b", ("own", "z1", "x0", "z3", "x1", "z2", "x3", "x2")),
+)
+WAITED = {GATE: ("z1", "x0"), LAST: ("z1", "x0", "x1", "z3", "z2", "x3", "x2")}
+
+
+def move(array, way):
+    if way == "y":
+        return lax.ppermute(array, "groups", [(0, 1), (1, 0)])
+    if way == "x":
+        pairs = [(i, i ^ 2) for i in range(4 * Z)]
+    elif way == "core":
+        pairs = [(i, i ^ 1) for i in range(4 * Z)]
+    else:
+        turn = 4 if way == "+" else -4
+        pairs = [(i, (i + turn) % (4 * Z)) for i in range(4 * Z)]
+    return lax.ppermute(array, "dp", pairs)
+
+
+def ring(node_rows, kept_counts, parents, cache_len, cache_kv, norm_gain, w_qkv, b_qkv):
+    depth = w_qkv.shape[0]
+    group = lax.axis_index("groups")
+    index = lax.axis_index("dp")
+    z, x, core = index // 4, (index // 2) % 2, index % 2
+    half = lax.dynamic_slice(w_qkv, (group * (depth // 2), SPLIT), (depth // 2, w_qkv.shape[1] - SPLIT))
+    first = w_qkv[:, :SPLIT]
+    tables = tree_tables(parents, cache_len)
+    normed, copy = normalize_both(node_rows, move(node_rows, "core"), norm_gain, core, half, tables)
+    pieces = {("a", "own"): w_qkv[:, SPLIT:], ("a", "z0"): half, ("a", "w0"): copy, ("b", "own"): first, ("b", "z0"): first}
+
+    def place(name, chunk):
+        if name == "own":
+            return 2 * z + x
+        side = 1 - group if name[0] == "y" else group
+        chip = 2 * ((z - int(name[-1])) % Z) + (1 - x if "x" in name else x)
+        return 2 * chip + side if chunk == "a" else chip
+
+    sums = {"a": None, "b": None}
+    for line in PLAN:
+        if isinstance(line, tuple):
+            chunk, names = line
+            batch = [(pieces[chunk, name], place(name, chunk)) for name in names]
+            copied = first if line == GATE else None
+            unread = [pieces["b", name] for name in WAITED.get(line, ())]
+            own_sum, other_sum, *copied = accumulate(normed, batch, sums[chunk], copied, unread)
+            sums[chunk] = own_sum, other_sum
+            if copied:
+                pieces["b", "w0"] = copied[0]
+        else:
+            chunk, way, sent, received = line.split()
+            pieces[chunk, received] = move(pieces[chunk, sent], way)
+
+    parts = [part for chunk in "ba" for part in (sums[chunk][0], move(sums[chunk][1], "core"))]
+    return attend_sums(parts, b_qkv.reshape(1, -1), tables, kept_counts, cache_len, cache_kv)
+
+
 def on_device(node_rows, kept_counts, parents, cache_len, cache_kv, norm_gain, w_qkv, b_qkv):
+    devices = lax.axis_size("dp")
+    if devices == 4 * Z and w_qkv.shape[0] % 512 == 0:
+        return ring(node_rows, kept_counts, parents, cache_len, cache_kv, norm_gain, w_qkv, b_qkv)
     weights = lax.all_gather(w_qkv, "dp", axis=0, tiled=True)
     normed = normalize(node_rows, norm_gain)
     tables = tree_tables(parents, cache_len)

time: 161 us -> 150 us (0.932)
  waiting for transfers between devices: 92.8 us -> 39 us
  Pallas kernels: 33.7 us -> 66.9 us
  starting transfers between devices: 0.01 us -> 28.7 us
  other arithmetic: 17.2 us -> 3.43 us
  between operations: 13.5 us -> 0.21 us
  local copies, waits for them, and re-layouts: 0.72 us -> 7.24 us
    all_gather x1 -> x0, waiting for transfers between devices: 92.1 us -> none  [on_device(): weights = lax.all_gather(w_qkv, 'dp', axis=0, tiled=True)]
    ppermute x0 -> x24, waiting for transfers between devices: none -> 39 us  [the longest x17 32.3 us: move(): return lax.ppermute(array, 'dp', pairs)]
    pallas_call x2 -> x6, Pallas kernels: 33.7 us -> 66.9 us  [the longest x4 36.5 us: accumulate(): pl.pallas_call(functools.partial(accumulate_kernel, count, len(unread), f...]
    ppermute x0 -> x24, starting transfers between devices: none -> 28.7 us  [the longest x17 21.1 us: move(): return lax.ppermute(array, 'dp', pairs)]
    convert_element_type x1 -> x0, other arithmetic: 10.1 us -> none  [normalize(): (values32 * lax.rsqrt(mean_square + EPSILON) * norm_gain).astype(jnp.bflo...]
    reduce_sum x1 -> x0, other arithmetic: 5.1 us -> none  [normalize(): mean_square = jnp.mean(values32 * values32, axis=-1, keepdims=True)]
    slice x0 -> x2, local copies, waits for them, and re-layouts: none -> 2.03 us  [the longest x1 1.04 us: ring(): first = w_qkv[:, :SPLIT]]
    another operation x0 -> x3, local copies, waits for them, and re-layouts: none -> 1.99 us  [accumulate(): places = jnp.stack([place for _, place in pieces]).astype(jnp.int32)]
  transfers between devices with their start and end apart: 1 -> 24, of which waited for: 1 -> 8; matrix products, arithmetic and copies ran while one was open for 13% -> 9% of each run, Pallas kernels for 0% -> 28%
where the time goes in v2:
time: 150 us
  Pallas kernels  66.9 us (45%)
  waiting for transfers between devices  39 us (26%)
  starting transfers between devices  28.7 us (19%)
  local copies, waits for them, and re-layouts  7.24 us (5%)
  matrix products  4.02 us (3%)
  other arithmetic  3.43 us (2%)
    pallas_call x4, Pallas kernels, accumulate(): pl.pallas_call(functools.partial(accumulate_kernel, count, len(unread), f...  36.5 us
    ppermute x17, waiting for transfers between devices, move(): return lax.ppermute(array, 'dp', pairs)  32.3 us
    ppermute x17, starting transfers between devices, move(): return lax.ppermute(array, 'dp', pairs)  21.1 us
    pallas_call x1, Pallas kernels, attend_sums(): pl.pallas_call(heads_kernel, out_shape=jax.ShapeDtypeStruct((rows, GROUP...  16.4 us
    pallas_call x1, Pallas kernels, normalize_both(): pl.pallas_call(functools.partial(norm_kernel, steps), out_shape=(jax.Shap...  14 us
    ppermute x7, starting transfers between devices, move(): return lax.ppermute(array, 'groups', [(0, 1), (1, 0)])  7.6 us
    ppermute x7, waiting for transfers between devices, move(): return lax.ppermute(array, 'groups', [(0, 1), (1, 0)])  6.63 us
    dot_general x4, matrix products, tree_tables(): jnp.einsum('rij,rjk->rik', reached, reached, preferred_element_type=jnp.f...  4.02 us
  transfers between devices with their start and end apart: 24, of which 8 were waited for; matrix products, arithmetic and copies ran while one was open for 9% of the time, Pallas kernels for 28%

profile of v2, /device:TPU:0, one launch (start us, length us, event | category | flops | bytes accessed | tf_op | source)
XLA Modules:
  0.0 149.5 jit_solution(6391354130168662496)
XLA Ops:
  0.0 0.5 collective-permute-start
  0.5 1.1 constant_dynamic-slice_fusion.w_ref
  1.5 0.0 copy-start.4
  1.5 2.6 %collective-permute-start.4 = (bf16[256,896]{1,0:T(8,128)(2,1)S(1)}, bf16[256,896]{1,0:T(8,128)(2,1)}, u32[]{:S(2)}, u32[]{:S(2)}) collective-permute-start(bf16[256,896]{1,0:T(8,128)(2,1)S(1)} %constant_dynamic-slice_fusion.w_ref), channel_id=1, source_target_pairs={{0,4},{1,5},{2,6},{3,7},{4,8},{5,9},{6,10},{7,11},{8,12},{9,13},{1... | collective-permute-start | bytes 1376264 | tf_op jit(solution)/shard_map/ppermute | solution.py:360
  4.2 1.5 collective-permute-start.3
  5.6 1.0 slice.6.refs_14_.refs_8_
  6.7 1.6 %collective-permute-start.1 = (bf16[512,384]{1,0:T(8,128)(2,1)S(1)}, bf16[512,384]{1,0:T(8,128)(2,1)S(1)}, u32[]{:S(2)}, u32[]{:S(2)}) collective-permute-start(bf16[512,384]{1,0:T(8,128)(2,1)S(1)} %slice.6.refs_14_.refs_8_), channel_id=1, source_target_pairs={{0,4},{1,5},{2,6},{3,7},{4,8},{5,9},{6,10},{7,11},{8,12},{9,13},{1... | collective-permute-start | bytes 1179656 | tf_op jit(solution)/shard_map/ppermute | solution.py:360
  8.3 0.5 collective-permute-start.2
  8.9 0.7 convert_element_type.39
  9.5 1.7 %fusion.1 = bf16[2,256,256]{2,1,0:T(8,128)(2,1)S(1)} fusion(s32[2,256]{1,0:T(2,128)} %param.10, pred[256]{0:T(512)(128)(4,1)S(1)} %iota_compare_fusion.2, pred[256,256]{1,0:T(8,128)(4,1)S(1)} %iota_compare_fusion.1), kind=kOutput, calls=%fused_computation.9 | convolution fusion | flops 135135232 | bytes 329984 | tf_op jit(solution)/shard_map/rij,rjk->rik/dot_general | solution.py:31
  11.3 0.5 fusion.3
  11.8 0.5 fusion.5
  12.3 1.3 convert_reduce_fusion
  13.6 0.1 add_add_fusion
  13.7 12.1 %collective-permute-done.1.refs_12_.refs_9_.refs_8_ = bf16[512,384]{1,0:T(8,128)(2,1)S(1)} collective-permute-done((bf16[512,384]{1,0:T(8,128)(2,1)S(1)}, bf16[512,384]{1,0:T(8,128)(2,1)S(1)}, u32[]{:S(2)}, u32[]{:S(2)}) %collective-permute-start.1) | collective-permute-done | bytes 393248 | tf_op jit(solution)/shard_map/ppermute | solution.py:360
  25.8 0.0 collective-permute-start.10
  25.8 1.0 fusion.22
  26.8 0.0 collective-permute-done.4.refs_8_
  26.8 1.6 %collective-permute-start.5 = (bf16[256,896]{1,0:T(8,128)(2,1)}, bf16[256,896]{1,0:T(8,128)(2,1)}, u32[]{:S(2)}, u32[]{:S(2)}) collective-permute-start(bf16[256,896]{1,0:T(8,128)(2,1)} %collective-permute-done.4.refs_8_), channel_id=1, source_target_pairs={{0,2},{1,3},{2,0},{3,1},{4,6},{5,7},{6,4},{7,5},{8,10},{9,11},{10,... | collective-permute-start | bytes 1376264 | tf_op jit(solution)/shard_map/ppermute | solution.py:360
  28.4 1.0 pad_maximum_fusion
  29.4 1.5 %collective-permute-start.7 = (bf16[256,896]{1,0:T(8,128)(2,1)}, bf16[256,896]{1,0:T(8,128)(2,1)}, u32[]{:S(2)}, u32[]{:S(2)}) collective-permute-start(bf16[256,896]{1,0:T(8,128)(2,1)} %collective-permute-done.4.refs_8_), channel_id=1, source_target_pairs={{0,16},{16,0},{1,17},{17,1},{2,18},{18,2},{3,19},{19,3},{4,20},{20... | collective-permute-start | bytes 1376264 | tf_op jit(solution)/shard_map/ppermute | solution.py:352
  30.9 14.0 %shard_map.82 = (bf16[1024,4096]{1,0:T(8,128)(2,1)}, bf16[256,896]{1,0:T(8,128)(2,1)}) custom-call(s32[1]{0:T(128)} %bitcast.8.core_ref, bf16[512,8192]{1,0:T(8,128)(2,1)} %x_ref.1, bf16[512,8192]{1,0:T(8,128)(2,1)} %collective-permute-done.other_ref, f32[1,8192]{1,0:T(1,128)} %bitcast.30, bf16[256,896]{1,0:T(8,128)(2,1)} %copy-done.4, ...), custom_call_target="tpu_custom_call" | custom-call | flops 33554432 | bytes 25165824 | tf_op jit(solution)/shard_map/pallas_call | solution.py:179
  44.9 0.0 collective-permute-done.2.refs_13_.refs_10_.refs_9_
  44.9 1.3 collective-permute-start.14
  46.3 2.6 %collective-permute-start.16 = (bf16[256,896]{1,0:T(8,128)(2,1)}, bf16[256,896]{1,0:T(8,128)(2,1)S(1)}, u32[]{:S(2)}, u32[]{:S(2)}) collective-permute-start(bf16[256,896]{1,0:T(8,128)(2,1)} %get-tuple-element.20), channel_id=1, source_target_pairs={{0,12},{1,13},{2,14},{3,15},{4,0},{5,1},{6,2},{7,3},{8,4},{9,5},{1... | collective-permute-start | bytes 1376264 | tf_op jit(solution)/shard_map/ppermute | solution.py:360
  48.9 0.5 collective-permute-start.6
  49.4 0.0 collective-permute-done.5.refs_9_
  49.4 0.5 collective-permute-start.9
  49.9 1.0 slice.7.refs_6_
  50.9 0.7 stack.93.place_ref
  51.6 0.0 collective-permute-done.7.refs_11_
  51.6 1.5 %collective-permute-start.22 = (bf16[256,896]{1,0:T(8,128)(2,1)}, bf16[256,896]{1,0:T(8,128)(2,1)S(1)}, u32[]{:S(2)}, u32[]{:S(2)}) collective-permute-start(bf16[256,896]{1,0:T(8,128)(2,1)} %collective-permute-done.5.refs_9_), channel_id=1, source_target_pairs={{0,16},{16,0},{1,17},{17,1},{2,18},{18,2},{3,19},{19,3},{4,20},{20... | collective-permute-start | bytes 1376264 | tf_op jit(solution)/shard_map/ppermute | solution.py:352
  53.1 7.5 %collective-permute-done.14.refs_5_ = bf16[256,896]{1,0:T(8,128)(2,1)} collective-permute-done((bf16[256,896]{1,0:T(8,128)(2,1)}, bf16[256,896]{1,0:T(8,128)(2,1)}, u32[]{:S(2)}, u32[]{:S(2)}) %collective-permute-start.14) | collective-permute-done | bytes 458784 | tf_op jit(solution)/shard_map/ppermute | solution.py:360
  60.6 0.5 collective-permute-start.19
  61.1 6.3 %collective-permute-done.16.refs_6_ = bf16[256,896]{1,0:T(8,128)(2,1)S(1)} collective-permute-done((bf16[256,896]{1,0:T(8,128)(2,1)}, bf16[256,896]{1,0:T(8,128)(2,1)S(1)}, u32[]{:S(2)}, u32[]{:S(2)}) %collective-permute-start.16) | collective-permute-done | bytes 458784 | tf_op jit(solution)/shard_map/ppermute | solution.py:360
  67.4 0.5 collective-permute-start.17
  67.9 0.5 collective-permute-start.21
  68.4 9.6 %shard_map.83 = (f32[512,896]{1,0:T(8,128)}, f32[512,896]{1,0:T(8,128)}, bf16[512,384]{1,0:T(8,128)(2,1)}) custom-call(s32[6]{0:T(128)} %stack.93.place_ref, bf16[1024,4096]{1,0:T(8,128)(2,1)} %get-tuple-element.16.refs_0_.refs_1_.refs_2_.refs_3_.refs_4_.refs_5_.refs_6_.refs_7_, ...), custom_call_target="tpu_custom_call" | custom-call | flops 3288334336 | bytes 10551296 | tf_op jit(solution)/shard_map/pallas_call | solution.py:242
  78.1 4.7 %collective-permute-start.8 = (bf16[512,384]{1,0:T(8,128)(2,1)}, bf16[512,384]{1,0:T(8,128)(2,1)S(1)}, u32[]{:S(2)}, u32[]{:S(2)}) collective-permute-start(bf16[512,384]{1,0:T(8,128)(2,1)} %get-tuple-element.17), channel_id=1, source_target_pairs={{0,12},{1,13},{2,14},{3,15},{4,0},{5,1},{6,2},{7,3},{8,4},{9,5},{1... | collective-permute-start | bytes 1179656 | tf_op jit(solution)/shard_map/ppermute | solution.py:360
  82.8 0.0 collective-permute-done.22.refs_9_
  82.8 1.5 %collective-permute-start.15 = (bf16[256,896]{1,0:T(8,128)(2,1)}, bf16[256,896]{1,0:T(8,128)(2,1)}, u32[]{:S(2)}, u32[]{:S(2)}) collective-permute-start(bf16[256,896]{1,0:T(8,128)(2,1)} %collective-permute-done.14.refs_5_), channel_id=1, source_target_pairs={{0,16},{16,0},{1,17},{17,1},{2,18},{18,2},{3,19},{19,3},{4,20},{20... | collective-permute-start | bytes 1376264 | tf_op jit(solution)/shard_map/ppermute | solution.py:352
  84.3 0.5 collective-permute-start.20
  84.8 0.0 collective-permute-done.17.refs_7_
  84.8 1.5 %collective-permute-start.18 = (bf16[256,896]{1,0:T(8,128)(2,1)S(1)}, bf16[256,896]{1,0:T(8,128)(2,1)}, u32[]{:S(2)}, u32[]{:S(2)}) collective-permute-start(bf16[256,896]{1,0:T(8,128)(2,1)S(1)} %collective-permute-done.17.refs_7_), channel_id=1, source_target_pairs={{0,16},{16,0},{1,17},{17,1},{2,18},{18,2},{3,19},{19,3},{4,20},{20... | collective-permute-start | bytes 1376264 | tf_op jit(solution)/shard_map/ppermute | solution.py:352
  86.3 2.7 %collective-permute-done.8.refs_11_ = bf16[512,384]{1,0:T(8,128)(2,1)S(1)} collective-permute-done((bf16[512,384]{1,0:T(8,128)(2,1)}, bf16[512,384]{1,0:T(8,128)(2,1)S(1)}, u32[]{:S(2)}, u32[]{:S(2)}) %collective-permute-start.8) | collective-permute-done | bytes 393248 | tf_op jit(solution)/shard_map/ppermute | solution.py:360
  89.1 1.4 collective-permute-start.12
  90.5 0.0 collective-permute-done.21.refs_8_
  90.5 0.7 collective-permute-start.11
  91.1 0.7 stack.104.place_ref
  91.8 0.7 pad_add_fusion.place_ref
  92.4 8.7 %shard_map.85 = (f32[512,896]{1,0:T(8,128)}, f32[512,896]{1,0:T(8,128)}) custom-call(s32[5]{0:T(128)} %stack.104.place_ref, bf16[1024,4096]{1,0:T(8,128)(2,1)} %get-tuple-element.16.refs_0_.refs_1_.refs_2_.refs_3_.refs_4_.refs_5_.refs_6_.refs_7_, ...), custom_call_target="tpu_custom_call", output_to_operand_aliasing={{0}: (11, {}), {1}: (12, {})} | custom-call | flops 2348810240 | bytes 12255232 | tf_op jit(solution)/shard_map/pallas_call | solution.py:242
  101.2 0.0 collective-permute-done.12.refs_15_.refs_14_
  101.2 3.9 %collective-permute-done.20.refs_7_ = bf16[256,896]{1,0:T(8,128)(2,1)} collective-permute-done((bf16[256,896]{1,0:T(8,128)(2,1)S(1)}, bf16[256,896]{1,0:T(8,128)(2,1)}, u32[]{:S(2)}, u32[]{:S(2)}) %collective-permute-start.20) | collective-permute-done | bytes 458784 | tf_op jit(solution)/shard_map/ppermute | solution.py:352
  105.1 2.2 %collective-permute-done.11.refs_14_.refs_13_ = bf16[512,384]{1,0:T(8,128)(2,1)S(1)} collective-permute-done((bf16[512,384]{1,0:T(8,128)(2,1)S(1)}, bf16[512,384]{1,0:T(8,128)(2,1)S(1)}, u32[]{:S(2)}, u32[]{:S(2)}) %collective-permute-start.11) | collective-permute-done | bytes 393248 | tf_op jit(solution)/shard_map/ppermute | solution.py:360
  107.3 2.7 %collective-permute-done.18.refs_5_ = bf16[256,896]{1,0:T(8,128)(2,1)} collective-permute-done((bf16[256,896]{1,0:T(8,128)(2,1)S(1)}, bf16[256,896]{1,0:T(8,128)(2,1)}, u32[]{:S(2)}, u32[]{:S(2)}) %collective-permute-start.18) | collective-permute-done | bytes 458784 | tf_op jit(solution)/shard_map/ppermute | solution.py:352
  110.0 8.1 %shard_map.86 = (f32[512,896]{1,0:T(8,128)}, f32[512,896]{1,0:T(8,128)}) custom-call(s32[4]{0:T(128)} %pad_add_fusion.place_ref, bf16[1024,4096]{1,0:T(8,128)(2,1)} %get-tuple-element.16.refs_0_.refs_1_.refs_2_.refs_3_.refs_4_.refs_5_.refs_6_.refs_7_, ...), custom_call_target="tpu_custom_call", output_to_operand_aliasing={{0}: (16, {}), {1}: (17, {})} | custom-call | flops 1879048192 | bytes 11272192 | tf_op jit(solution)/shard_map/pallas_call | solution.py:242
  118.1 0.7 stack.87.place_ref
  118.8 10.1 %shard_map.84 = (f32[512,384]{1,0:T(8,128)}, f32[512,384]{1,0:T(8,128)}) custom-call(s32[8]{0:T(128)} %stack.87.place_ref, bf16[1024,4096]{1,0:T(8,128)(2,1)} %get-tuple-element.16.refs_0_.refs_1_.refs_2_.refs_3_.refs_4_.refs_5_.refs_6_.refs_7_, bf16[1024,4096]{1,0:T(8,128)(2,1)} %get-tuple-element.16.refs_0_.refs_1_.refs_2_.refs_3_.refs_4_.refs_5_.refs_6_.refs_7_, ...), custom_call_target="tpu_custom_call" | custom-call | flops 3221225472 | bytes 13107200 | tf_op jit(solution)/shard_map/pallas_call | solution.py:242
  128.9 0.6 collective-permute-start.13
  129.5 0.6 reshape.55.b_ref
  130.1 1.5 %collective-permute-done.13.got_b = f32[512,384]{1,0:T(8,128)S(1)} collective-permute-done((f32[512,384]{1,0:T(8,128)}, f32[512,384]{1,0:T(8,128)S(1)}, u32[]{:S(2)}, u32[]{:S(2)}) %collective-permute-start.13) | collective-permute-done | bytes 786464 | tf_op jit(solution)/shard_map/ppermute | solution.py:360
  131.6 0.9 copy-done.16
  132.5 0.6 copy-done.15
  133.1 16.4 %shard_map.87 = bf16[512,1024]{1,0:T(8,128)(2,1)} custom-call(s32[2]{0:T(128)} %kept_ref.1, s32[2]{0:T(128)} %len_ref.1, f32[512,384]{1,0:T(8,128)} %get-tuple-element.18.own_b, f32[512,384]{1,0:T(8,128)} %copy-done.16, f32[512,896]{1,0:T(8,128)} %get-tuple-element.25.own_a, f32[512,896]{1,0:T(8,128)} %copy-done.15, f32[1,1280]{1,0:T(1,128)} %reshape.55.b_ref, ...), custom_call_target="tpu_custom_call" | custom-call | flops 2684354560 | bytes 20971520 | tf_op jit(solution)/shard_map/pallas_call | solution.py:312
  (43 shorter events, 0.1 us)
Async XLA Ops:
  0.0 29.4 %collective-permute-start = (bf16[512,8192]{1,0:T(8,128)(2,1)}, bf16[512,8192]{1,0:T(8,128)(2,1)}, u32[]{:S(2)}, u32[]{:S(2)}) collective-permute-start(bf16[512,8192]{1,0:T(8,128)(2,1)} %x_ref.1), channel_id=1, source_target_pairs={{0,1},{1,0},{2,3},{3,2},{4,5},{5,4},{6,7},{7,6},{8,9},{9,8},{10,11... | collective-permute-start | bytes 25165832 | tf_op jit(solution)/shard_map/ppermute | solution.py:360
  1.5 10.8 %copy-start.4 = (bf16[256,896]{1,0:T(8,128)(2,1)}, bf16[256,896]{1,0:T(8,128)(2,1)S(1)}, u32[]{:S(2)}) copy-start(bf16[256,896]{1,0:T(8,128)(2,1)S(1)} %constant_dynamic-slice_fusion.w_ref) | copy-start | bytes 1376260
  1.5 25.3 %collective-permute-start.4 = (bf16[256,896]{1,0:T(8,128)(2,1)S(1)}, bf16[256,896]{1,0:T(8,128)(2,1)}, u32[]{:S(2)}, u32[]{:S(2)}) collective-permute-start(bf16[256,896]{1,0:T(8,128)(2,1)S(1)} %constant_dynamic-slice_fusion.w_ref), channel_id=1, source_target_pairs={{0,4},{1,5},{2,6},{3,7},{4,8},{5,9},{6,10},{7,11},{8,12},{9,13},{1... | collective-permute-start | bytes 1376264 | tf_op jit(solution)/shard_map/ppermute | solution.py:360
  4.2 42.1 %collective-permute-start.3 = (bf16[256,896]{1,0:T(8,128)(2,1)S(1)}, bf16[256,896]{1,0:T(8,128)(2,1)}, u32[]{:S(2)}, u32[]{:S(2)}) collective-permute-start(bf16[256,896]{1,0:T(8,128)(2,1)S(1)} %constant_dynamic-slice_fusion.w_ref), channel_id=1, source_target_pairs={{0,2},{1,3},{2,0},{3,1},{4,6},{5,7},{6,4},{7,5},{8,10},{9,11},{10,... | collective-permute-start | bytes 1376264 | tf_op jit(solution)/shard_map/ppermute | solution.py:360
  6.7 6.9 %copy-start.2 = (bf16[512,384]{1,0:T(8,128)(2,1)}, bf16[512,384]{1,0:T(8,128)(2,1)S(1)}, u32[]{:S(2)}) copy-start(bf16[512,384]{1,0:T(8,128)(2,1)S(1)} %slice.6.refs_14_.refs_8_) | copy-start | bytes 1179652
  6.7 19.1 %collective-permute-start.1 = (bf16[512,384]{1,0:T(8,128)(2,1)S(1)}, bf16[512,384]{1,0:T(8,128)(2,1)S(1)}, u32[]{:S(2)}, u32[]{:S(2)}) collective-permute-start(bf16[512,384]{1,0:T(8,128)(2,1)S(1)} %slice.6.refs_14_.refs_8_), channel_id=1, source_target_pairs={{0,4},{1,5},{2,6},{3,7},{4,8},{5,9},{6,10},{7,11},{8,12},{9,13},{1... | collective-permute-start | bytes 1179656 | tf_op jit(solution)/shard_map/ppermute | solution.py:360
  8.3 36.6 %collective-permute-start.2 = (bf16[512,384]{1,0:T(8,128)(2,1)S(1)}, bf16[512,384]{1,0:T(8,128)(2,1)S(1)}, u32[]{:S(2)}, u32[]{:S(2)}) collective-permute-start(bf16[512,384]{1,0:T(8,128)(2,1)S(1)} %slice.6.refs_14_.refs_8_), channel_id=1, source_target_pairs={{0,2},{1,3},{2,0},{3,1},{4,6},{5,7},{6,4},{7,5},{8,10},{9,11},{10,... | collective-permute-start | bytes 1179656 | tf_op jit(solution)/shard_map/ppermute | solution.py:360
  25.8 23.6 %copy-start = (bf16[512,384]{1,0:T(8,128)(2,1)}, bf16[512,384]{1,0:T(8,128)(2,1)S(1)}, u32[]{:S(2)}) copy-start(bf16[512,384]{1,0:T(8,128)(2,1)S(1)} %collective-permute-done.1.refs_12_.refs_9_.refs_8_) | copy-start | bytes 1179652
  25.8 23.1 %collective-permute-start.10 = (bf16[512,384]{1,0:T(8,128)(2,1)S(1)}, bf16[512,384]{1,0:T(8,128)(2,1)S(1)}, u32[]{:S(2)}, u32[]{:S(2)}) collective-permute-start(bf16[512,384]{1,0:T(8,128)(2,1)S(1)} %collective-permute-done.1.refs_12_.refs_9_.refs_8_), channel_id=1, source_target_pairs={{0,4},{1,5},{2,6},{3,7},{4,8},{5,9},{6,10},{7,11},{8,12},{9,13},{1... | collective-permute-start | bytes 1179656 | tf_op jit(solution)/shard_map/ppermute | solution.py:360
  26.8 22.6 %collective-permute-start.5 = (bf16[256,896]{1,0:T(8,128)(2,1)}, bf16[256,896]{1,0:T(8,128)(2,1)}, u32[]{:S(2)}, u32[]{:S(2)}) collective-permute-start(bf16[256,896]{1,0:T(8,128)(2,1)} %collective-permute-done.4.refs_8_), channel_id=1, source_target_pairs={{0,2},{1,3},{2,0},{3,1},{4,6},{5,7},{6,4},{7,5},{8,10},{9,11},{10,... | collective-permute-start | bytes 1376264 | tf_op jit(solution)/shard_map/ppermute | solution.py:360
  29.4 22.2 %collective-permute-start.7 = (bf16[256,896]{1,0:T(8,128)(2,1)}, bf16[256,896]{1,0:T(8,128)(2,1)}, u32[]{:S(2)}, u32[]{:S(2)}) collective-permute-start(bf16[256,896]{1,0:T(8,128)(2,1)} %collective-permute-done.4.refs_8_), channel_id=1, source_target_pairs={{0,16},{16,0},{1,17},{17,1},{2,18},{18,2},{3,19},{19,3},{4,20},{20... | collective-permute-start | bytes 1376264 | tf_op jit(solution)/shard_map/ppermute | solution.py:352
  30.9 19.0 %copy-start.3 = (bf16[512,1280]{1,0:T(8,128)(2,1)S(1)}, bf16[512,1280]{1,0:T(8,128)(2,1)}, u32[]{:S(2)}) copy-start(bf16[512,1280]{1,0:T(8,128)(2,1)} %param.14) | copy-start | bytes 3932164
  44.9 23.5 %copy-start.1 = (bf16[512,384]{1,0:T(8,128)(2,1)}, bf16[512,384]{1,0:T(8,128)(2,1)S(1)}, u32[]{:S(2)}) copy-start(bf16[512,384]{1,0:T(8,128)(2,1)S(1)} %collective-permute-done.2.refs_13_.refs_10_.refs_9_) | copy-start | bytes 1179652
  44.9 15.7 %collective-permute-start.14 = (bf16[256,896]{1,0:T(8,128)(2,1)}, bf16[256,896]{1,0:T(8,128)(2,1)}, u32[]{:S(2)}, u32[]{:S(2)}) collective-permute-start(bf16[256,896]{1,0:T(8,128)(2,1)} %collective-permute-done.4.refs_8_), channel_id=1, source_target_pairs={{0,4},{1,5},{2,6},{3,7},{4,8},{5,9},{6,10},{7,11},{8,12},{9,13},{1... | collective-permute-start | bytes 1376264 | tf_op jit(solution)/shard_map/ppermute | solution.py:360
  46.3 21.1 %collective-permute-start.16 = (bf16[256,896]{1,0:T(8,128)(2,1)}, bf16[256,896]{1,0:T(8,128)(2,1)S(1)}, u32[]{:S(2)}, u32[]{:S(2)}) collective-permute-start(bf16[256,896]{1,0:T(8,128)(2,1)} %get-tuple-element.20), channel_id=1, source_target_pairs={{0,12},{1,13},{2,14},{3,15},{4,0},{5,1},{6,2},{7,3},{8,4},{9,5},{1... | collective-permute-start | bytes 1376264 | tf_op jit(solution)/shard_map/ppermute | solution.py:360
  48.9 40.2 %copy-start.5 = (bf16[512,384]{1,0:T(8,128)(2,1)}, bf16[512,384]{1,0:T(8,128)(2,1)S(1)}, u32[]{:S(2)}) copy-start(bf16[512,384]{1,0:T(8,128)(2,1)S(1)} %collective-permute-done.10.refs_13_.refs_12_) | copy-start | bytes 1179652
  48.9 19.1 %collective-permute-start.6 = (bf16[256,896]{1,0:T(8,128)(2,1)}, bf16[256,896]{1,0:T(8,128)(2,1)}, u32[]{:S(2)}, u32[]{:S(2)}) collective-permute-start(bf16[256,896]{1,0:T(8,128)(2,1)} %collective-permute-done.3.refs_7_), channel_id=1, source_target_pairs={{0,16},{16,0},{1,17},{17,1},{2,18},{18,2},{3,19},{19,3},{4,20},{20... | collective-permute-start | bytes 1376264 | tf_op jit(solution)/shard_map/ppermute | solution.py:352
  49.4 28.6 %collective-permute-start.9 = (bf16[512,384]{1,0:T(8,128)(2,1)S(1)}, bf16[512,384]{1,0:T(8,128)(2,1)S(1)}, u32[]{:S(2)}, u32[]{:S(2)}) collective-permute-start(bf16[512,384]{1,0:T(8,128)(2,1)S(1)} %collective-permute-done.1.refs_12_.refs_9_.refs_8_), channel_id=1, source_target_pairs={{0,2},{1,3},{2,0},{3,1},{4,6},{5,7},{6,4},{7,5},{8,10},{9,11},{10,... | collective-permute-start | bytes 1179656 | tf_op jit(solution)/shard_map/ppermute | solution.py:360
  51.6 31.2 %collective-permute-start.22 = (bf16[256,896]{1,0:T(8,128)(2,1)}, bf16[256,896]{1,0:T(8,128)(2,1)S(1)}, u32[]{:S(2)}, u32[]{:S(2)}) collective-permute-start(bf16[256,896]{1,0:T(8,128)(2,1)} %collective-permute-done.5.refs_9_), channel_id=1, source_target_pairs={{0,16},{16,0},{1,17},{17,1},{2,18},{18,2},{3,19},{19,3},{4,20},{20... | collective-permute-start | bytes 1376264 | tf_op jit(solution)/shard_map/ppermute | solution.py:352
  60.6 23.7 %collective-permute-start.19 = (bf16[256,896]{1,0:T(8,128)(2,1)}, bf16[256,896]{1,0:T(8,128)(2,1)S(1)}, u32[]{:S(2)}, u32[]{:S(2)}) collective-permute-start(bf16[256,896]{1,0:T(8,128)(2,1)} %collective-permute-done.14.refs_5_), channel_id=1, source_target_pairs={{0,2},{1,3},{2,0},{3,1},{4,6},{5,7},{6,4},{7,5},{8,10},{9,11},{10,... | collective-permute-start | bytes 1376264 | tf_op jit(solution)/shard_map/ppermute | solution.py:360
  67.4 10.6 %copy-start.10 = (bf16[256,896]{1,0:T(8,128)(2,1)}, bf16[256,896]{1,0:T(8,128)(2,1)S(1)}, u32[]{:S(2)}) copy-start(bf16[256,896]{1,0:T(8,128)(2,1)S(1)} %collective-permute-done.16.refs_6_) | copy-start | bytes 1376260
  67.4 17.4 %collective-permute-start.17 = (bf16[256,896]{1,0:T(8,128)(2,1)S(1)}, bf16[256,896]{1,0:T(8,128)(2,1)S(1)}, u32[]{:S(2)}, u32[]{:S(2)}) collective-permute-start(bf16[256,896]{1,0:T(8,128)(2,1)S(1)} %collective-permute-done.16.refs_6_), channel_id=1, source_target_pairs={{0,2},{1,3},{2,0},{3,1},{4,6},{5,7},{6,4},{7,5},{8,10},{9,11},{10,... | collective-permute-start | bytes 1376264 | tf_op jit(solution)/shard_map/ppermute | solution.py:360
  67.9 22.5 %collective-permute-start.21 = (bf16[256,896]{1,0:T(8,128)(2,1)S(1)}, bf16[256,896]{1,0:T(8,128)(2,1)}, u32[]{:S(2)}, u32[]{:S(2)}) collective-permute-start(bf16[256,896]{1,0:T(8,128)(2,1)S(1)} %collective-permute-done.16.refs_6_), channel_id=1, source_target_pairs={{0,16},{16,0},{1,17},{17,1},{2,18},{18,2},{3,19},{19,3},{4,20},{20... | collective-permute-start | bytes 1376264 | tf_op jit(solution)/shard_map/ppermute | solution.py:352
  78.1 23.1 %copy-start.6 = (bf16[512,384]{1,0:T(8,128)(2,1)}, bf16[512,384]{1,0:T(8,128)(2,1)S(1)}, u32[]{:S(2)}) copy-start(bf16[512,384]{1,0:T(8,128)(2,1)S(1)} %collective-permute-done.9.refs_12_.refs_10_) | copy-start | bytes 1179652
  78.1 11.0 %collective-permute-start.8 = (bf16[512,384]{1,0:T(8,128)(2,1)}, bf16[512,384]{1,0:T(8,128)(2,1)S(1)}, u32[]{:S(2)}, u32[]{:S(2)}) collective-permute-start(bf16[512,384]{1,0:T(8,128)(2,1)} %get-tuple-element.17), channel_id=1, source_target_pairs={{0,12},{1,13},{2,14},{3,15},{4,0},{5,1},{6,2},{7,3},{8,4},{9,5},{1... | collective-permute-start | bytes 1179656 | tf_op jit(solution)/shard_map/ppermute | solution.py:360
  82.8 7.7 %copy-start.13 = (bf16[256,896]{1,0:T(8,128)(2,1)}, bf16[256,896]{1,0:T(8,128)(2,1)S(1)}, u32[]{:S(2)}) copy-start(bf16[256,896]{1,0:T(8,128)(2,1)S(1)} %collective-permute-done.22.refs_9_) | copy-start | bytes 1376260
  82.8 18.4 %collective-permute-start.15 = (bf16[256,896]{1,0:T(8,128)(2,1)}, bf16[256,896]{1,0:T(8,128)(2,1)}, u32[]{:S(2)}, u32[]{:S(2)}) collective-permute-start(bf16[256,896]{1,0:T(8,128)(2,1)} %collective-permute-done.14.refs_5_), channel_id=1, source_target_pairs={{0,16},{16,0},{1,17},{17,1},{2,18},{18,2},{3,19},{19,3},{4,20},{20... | collective-permute-start | bytes 1376264 | tf_op jit(solution)/shard_map/ppermute | solution.py:352
  84.3 16.8 %copy-start.11 = (bf16[256,896]{1,0:T(8,128)(2,1)}, bf16[256,896]{1,0:T(8,128)(2,1)S(1)}, u32[]{:S(2)}) copy-start(bf16[256,896]{1,0:T(8,128)(2,1)S(1)} %collective-permute-done.19.refs_6_) | copy-start | bytes 1376260
  84.3 20.8 %collective-permute-start.20 = (bf16[256,896]{1,0:T(8,128)(2,1)S(1)}, bf16[256,896]{1,0:T(8,128)(2,1)}, u32[]{:S(2)}, u32[]{:S(2)}) collective-permute-start(bf16[256,896]{1,0:T(8,128)(2,1)S(1)} %collective-permute-done.19.refs_6_), channel_id=1, source_target_pairs={{0,16},{16,0},{1,17},{17,1},{2,18},{18,2},{3,19},{19,3},{4,20},{20... | collective-permute-start | bytes 1376264 | tf_op jit(solution)/shard_map/ppermute | solution.py:352
  84.8 7.6 %copy-start.12 = (bf16[256,896]{1,0:T(8,128)(2,1)}, bf16[256,896]{1,0:T(8,128)(2,1)S(1)}, u32[]{:S(2)}) copy-start(bf16[256,896]{1,0:T(8,128)(2,1)S(1)} %collective-permute-done.17.refs_7_) | copy-start | bytes 1376260
  84.8 25.2 %collective-permute-start.18 = (bf16[256,896]{1,0:T(8,128)(2,1)S(1)}, bf16[256,896]{1,0:T(8,128)(2,1)}, u32[]{:S(2)}, u32[]{:S(2)}) collective-permute-start(bf16[256,896]{1,0:T(8,128)(2,1)S(1)} %collective-permute-done.17.refs_7_), channel_id=1, source_target_pairs={{0,16},{16,0},{1,17},{17,1},{2,18},{18,2},{3,19},{19,3},{4,20},{20... | collective-permute-start | bytes 1376264 | tf_op jit(solution)/shard_map/ppermute | solution.py:352
  89.1 12.1 %copy-start.7 = (bf16[512,384]{1,0:T(8,128)(2,1)}, bf16[512,384]{1,0:T(8,128)(2,1)S(1)}, u32[]{:S(2)}) copy-start(bf16[512,384]{1,0:T(8,128)(2,1)S(1)} %collective-permute-done.8.refs_11_) | copy-start | bytes 1179652
  89.1 12.1 %collective-permute-start.12 = (bf16[512,384]{1,0:T(8,128)(2,1)S(1)}, bf16[512,384]{1,0:T(8,128)(2,1)S(1)}, u32[]{:S(2)}, u32[]{:S(2)}) collective-permute-start(bf16[512,384]{1,0:T(8,128)(2,1)S(1)} %collective-permute-done.10.refs_13_.refs_12_), channel_id=1, source_target_pairs={{0,2},{1,3},{2,0},{3,1},{4,6},{5,7},{6,4},{7,5},{8,10},{9,11},{10,... | collective-permute-start | bytes 1179656 | tf_op jit(solution)/shard_map/ppermute | solution.py:360
  90.5 16.8 %collective-permute-start.11 = (bf16[512,384]{1,0:T(8,128)(2,1)S(1)}, bf16[512,384]{1,0:T(8,128)(2,1)S(1)}, u32[]{:S(2)}, u32[]{:S(2)}) collective-permute-start(bf16[512,384]{1,0:T(8,128)(2,1)S(1)} %collective-permute-done.8.refs_11_), channel_id=1, source_target_pairs={{0,2},{1,3},{2,0},{3,1},{4,6},{5,7},{6,4},{7,5},{8,10},{9,11},{10,... | collective-permute-start | bytes 1179656 | tf_op jit(solution)/shard_map/ppermute | solution.py:360
  101.2 8.8 %copy-start.8 = (bf16[512,384]{1,0:T(8,128)(2,1)}, bf16[512,384]{1,0:T(8,128)(2,1)S(1)}, u32[]{:S(2)}) copy-start(bf16[512,384]{1,0:T(8,128)(2,1)S(1)} %collective-permute-done.12.refs_15_.refs_14_) | copy-start | bytes 1179652
  107.3 2.7 %copy-start.9 = (bf16[512,384]{1,0:T(8,128)(2,1)}, bf16[512,384]{1,0:T(8,128)(2,1)S(1)}, u32[]{:S(2)}) copy-start(bf16[512,384]{1,0:T(8,128)(2,1)S(1)} %collective-permute-done.11.refs_14_.refs_13_) | copy-start | bytes 1179652
  118.1 13.5 %collective-permute-start.23 = (f32[512,896]{1,0:T(8,128)}, f32[512,896]{1,0:T(8,128)S(1)}, u32[]{:S(2)}, u32[]{:S(2)}) collective-permute-start(f32[512,896]{1,0:T(8,128)} %get-tuple-element.26), channel_id=1, source_target_pairs={{0,1},{1,0},{2,3},{3,2},{4,5},{5,4},{6,7},{7,6},{8,9},{9,8},{10,11... | collective-permute-start | bytes 5505032 | tf_op jit(solution)/shard_map/ppermute | solution.py:360
  118.8 10.7 %copy-start.14 = (f32[1280]{0:T(1024)S(1)}, f32[1280]{0:T(1024)}, u32[]{:S(2)}) copy-start(f32[1280]{0:T(1024)} %param.15) | copy-start | bytes 15364
  128.9 2.7 %collective-permute-start.13 = (f32[512,384]{1,0:T(8,128)}, f32[512,384]{1,0:T(8,128)S(1)}, u32[]{:S(2)}, u32[]{:S(2)}) collective-permute-start(f32[512,384]{1,0:T(8,128)} %get-tuple-element.19), channel_id=1, source_target_pairs={{0,1},{1,0},{2,3},{3,2},{4,5},{5,4},{6,7},{7,6},{8,9},{9,8},{10,11... | collective-permute-start | bytes 2359304 | tf_op jit(solution)/shard_map/ppermute | solution.py:360
  131.6 0.9 copy-start.16
  131.6 1.5 %copy-start.15 = (f32[512,896]{1,0:T(8,128)}, f32[512,896]{1,0:T(8,128)S(1)}, u32[]{:S(2)}) copy-start(f32[512,896]{1,0:T(8,128)S(1)} %collective-permute-done.23.got_a) | copy-start | bytes 5505028

commit v3 on v2

--- a/solution.py
+++ b/solution.py
@@ -333,13 +333,14 @@
 Z = 4
 CHIPS = 2 * Z
 SPLIT = 3 * HEAD
-NORM_LIMIT = DOT_LIMIT = HEADS_LIMIT = 60
-
-GATE = ("a", ("own", "x0", "z1", "x1", "yx0", "yz1"))
-MIDDLE = ("a", ("z2", "z3", "x3", "yz3", "yx1"))
+NORM_LIMIT = DOT_LIMIT = 60
+HEADS_LIMIT = 30
+
+GATE = ("a", ("own", "x0", "z1", "x1", "yx0", "yz1", "z3"))
+MIDDLE = ("a", ("z2", "x3", "yz3", "yx1"))
 LAST = ("a", ("yz2", "yx3", "x2", "yx2"))
 PLAN = (
-    "a + z0 z1", "a x z0 x0", "a x z1 x1", "a y z1 yz1", "a - w0 z3", "a + z1 z2", "a x z3 x3", "a y x0 yx0",
+    "a + z0 z1", "a x z0 x0", "a x z1 x1", "a y z1 yz1", "a - z0 z3", "a + z1 z2", "a x z3 x3", "a y x0 yx0",
     "b + z0 z1", "b x z0 x0", "a y z3 yz3", GATE, "b - w0 z3", "b x z1 x1", "a y x1 yx1", "b + z1 z2", "b x z3 x3",
     "a y z2 yz2", "a x z2 x2", "a y x3 yx3", "b x z2 x2", "a y x2 yx2",
     MIDDLE, LAST, ("b", ("own", "z1", "x0", "z3", "x1", "z2", "x3", "x2")),
@@ -368,8 +369,8 @@
     half = lax.dynamic_slice(w_qkv, (group * (depth // 2), SPLIT), (depth // 2, w_qkv.shape[1] - SPLIT))
     first = w_qkv[:, :SPLIT]
     tables = tree_tables(parents, cache_len)
-    normed, copy = normalize_both(node_rows, move(node_rows, "core"), norm_gain, core, half, tables)
-    pieces = {("a", "own"): w_qkv[:, SPLIT:], ("a", "z0"): half, ("a", "w0"): copy, ("b", "own"): first, ("b", "z0"): first}
+    normed, copy = normalize_both(node_rows, move(node_rows, "core"), norm_gain, core, first, tables)
+    pieces = {("a", "own"): w_qkv[:, SPLIT:], ("a", "z0"): half, ("b", "own"): first, ("b", "z0"): copy}
 
     def place(name, chunk):
         if name == "own":

time: 150 us -> 139 us (0.927)
  waiting for transfers between devices: 39 us -> 22.2 us
  starting transfers between devices: 28.7 us -> 36.5 us
    ppermute x17, waiting for transfers between devices: 32.3 us -> 14.9 us  [move(): return lax.ppermute(array, 'dp', pairs)]
    ppermute x17, starting transfers between devices: 21.1 us -> 27.6 us  [move(): return lax.ppermute(array, 'dp', pairs)]
  transfers between devices with their start and end apart: 24 -> 24, of which waited for: 8 -> 7; matrix products, arithmetic and copies ran while one was open for 9% -> 8% of each run, Pallas kernels for 28% -> 31%
where the time goes in v3:
time: 139 us
  Pallas kernels  66 us (47%)
  starting transfers between devices  36.5 us (26%)
  waiting for transfers between devices  22.2 us (16%)
  local copies, waits for them, and re-layouts  6.13 us (4%)
  matrix products  4.01 us (3%)
  other arithmetic  3.42 us (2%)
    pallas_call x4, Pallas kernels, accumulate(): pl.pallas_call(functools.partial(accumulate_kernel, count, len(unread), f...  36.8 us
    ppermute x17, starting transfers between devices, move(): return lax.ppermute(array, 'dp', pairs)  27.6 us
    pallas_call x1, Pallas kernels, attend_sums(): pl.pallas_call(heads_kernel, out_shape=jax.ShapeDtypeStruct((rows, GROUP...  15.1 us
    ppermute x17, waiting for transfers between devices, move(): return lax.ppermute(array, 'dp', pairs)  14.9 us
    pallas_call x1, Pallas kernels, normalize_both(): pl.pallas_call(functools.partial(norm_kernel, steps), out_shape=(jax.Shap...  14.2 us
    ppermute x7, starting transfers between devices, move(): return lax.ppermute(array, 'groups', [(0, 1), (1, 0)])  8.9 us
    ppermute x7, waiting for transfers between devices, move(): return lax.ppermute(array, 'groups', [(0, 1), (1, 0)])  7.33 us
    dot_general x4, matrix products, tree_tables(): jnp.einsum('rij,rjk->rik', reached, reached, preferred_element_type=jnp.f...  4.01 us
  transfers between devices with their start and end apart: 24, of which 7 were waited for; matrix products, arithmetic and copies ran while one was open for 8% of the time, Pallas kernels for 31%

profile of v3, /device:TPU:0, one launch (start us, length us, event | category | flops | bytes accessed | tf_op | source)
XLA Modules:
  0.0 138.5 jit_solution(15110790583293392835)
XLA Ops:
  0.0 0.5 collective-permute-start
  0.5 1.1 constant_dynamic-slice_fusion
  1.5 2.6 %collective-permute-start.4 = (bf16[256,896]{1,0:T(8,128)(2,1)S(1)}, bf16[256,896]{1,0:T(8,128)(2,1)}, u32[]{:S(2)}, u32[]{:S(2)}) collective-permute-start(bf16[256,896]{1,0:T(8,128)(2,1)S(1)} %constant_dynamic-slice_fusion), channel_id=1, source_target_pairs={{0,4},{1,5},{2,6},{3,7},{4,8},{5,9},{6,10},{7,11},{8,12},{9,13},{1... | collective-permute-start | bytes 1376264 | tf_op jit(solution)/shard_map/ppermute | solution.py:361
  4.1 2.1 %collective-permute-start.8 = (bf16[256,896]{1,0:T(8,128)(2,1)S(1)}, bf16[256,896]{1,0:T(8,128)(2,1)S(1)}, u32[]{:S(2)}, u32[]{:S(2)}) collective-permute-start(bf16[256,896]{1,0:T(8,128)(2,1)S(1)} %constant_dynamic-slice_fusion), channel_id=1, source_target_pairs={{0,12},{1,13},{2,14},{3,15},{4,0},{5,1},{6,2},{7,3},{8,4},{9,5},{1... | collective-permute-start | bytes 1376264 | tf_op jit(solution)/shard_map/ppermute | solution.py:361
  6.2 1.6 %collective-permute-start.3 = (bf16[256,896]{1,0:T(8,128)(2,1)S(1)}, bf16[256,896]{1,0:T(8,128)(2,1)}, u32[]{:S(2)}, u32[]{:S(2)}) collective-permute-start(bf16[256,896]{1,0:T(8,128)(2,1)S(1)} %constant_dynamic-slice_fusion), channel_id=1, source_target_pairs={{0,2},{1,3},{2,0},{3,1},{4,6},{5,7},{6,4},{7,5},{8,10},{9,11},{10,... | collective-permute-start | bytes 1376264 | tf_op jit(solution)/shard_map/ppermute | solution.py:361
  7.9 1.7 %fusion.1 = bf16[2,256,256]{2,1,0:T(8,128)(2,1)S(1)} fusion(s32[2,256]{1,0:T(2,128)} %param.10, pred[256]{0:T(512)(128)(4,1)S(1)} %iota_compare_fusion.2, pred[256,256]{1,0:T(8,128)(4,1)S(1)} %iota_compare_fusion.1), kind=kOutput, calls=%fused_computation.9 | convolution fusion | flops 135135232 | bytes 329984 | tf_op jit(solution)/shard_map/rij,rjk->rik/dot_general | solution.py:31
  9.6 0.0 copy-start.7
  9.6 0.5 fusion.3
  10.1 0.5 fusion.5
  10.7 0.0 copy-start.10
  10.7 1.3 convert_reduce_fusion
  12.0 0.1 add_add_fusion
  12.0 5.6 %collective-permute-done.4.refs_9_ = bf16[256,896]{1,0:T(8,128)(2,1)} collective-permute-done((bf16[256,896]{1,0:T(8,128)(2,1)S(1)}, bf16[256,896]{1,0:T(8,128)(2,1)}, u32[]{:S(2)}, u32[]{:S(2)}) %collective-permute-start.4) | collective-permute-done | bytes 458784 | tf_op jit(solution)/shard_map/ppermute | solution.py:361
  17.7 1.6 %collective-permute-start.5 = (bf16[256,896]{1,0:T(8,128)(2,1)}, bf16[256,896]{1,0:T(8,128)(2,1)}, u32[]{:S(2)}, u32[]{:S(2)}) collective-permute-start(bf16[256,896]{1,0:T(8,128)(2,1)} %collective-permute-done.4.refs_9_), channel_id=1, source_target_pairs={{0,2},{1,3},{2,0},{3,1},{4,6},{5,7},{6,4},{7,5},{8,10},{9,11},{10,... | collective-permute-start | bytes 1376264 | tf_op jit(solution)/shard_map/ppermute | solution.py:361
  19.3 1.5 %collective-permute-start.7 = (bf16[256,896]{1,0:T(8,128)(2,1)}, bf16[256,896]{1,0:T(8,128)(2,1)}, u32[]{:S(2)}, u32[]{:S(2)}) collective-permute-start(bf16[256,896]{1,0:T(8,128)(2,1)} %collective-permute-done.4.refs_9_), channel_id=1, source_target_pairs={{0,16},{16,0},{1,17},{17,1},{2,18},{18,2},{3,19},{19,3},{4,20},{20... | collective-permute-start | bytes 1376264 | tf_op jit(solution)/shard_map/ppermute | solution.py:353
  20.8 0.0 collective-permute-done.3.refs_8_
  20.8 0.5 collective-permute-start.6
  21.4 1.0 fusion.22
  22.3 0.0 collective-permute-done.other_ref
  22.4 0.1 collective-permute-start.15
  22.4 1.0 pad_maximum_fusion
  23.4 0.8 slice.6.w_ref.refs_16_.refs_8_
  24.2 14.2 %shard_map.82 = (bf16[1024,4096]{1,0:T(8,128)(2,1)}, bf16[512,384]{1,0:T(8,128)(2,1)}) custom-call(s32[1]{0:T(128)} %bitcast.8.core_ref, bf16[512,8192]{1,0:T(8,128)(2,1)} %x_ref.1, bf16[512,8192]{1,0:T(8,128)(2,1)} %collective-permute-done.other_ref, f32[1,8192]{1,0:T(1,128)} %bitcast.30, bf16[512,384]{1,0:T(8,128)(2,1)} %slice.6.w_ref.refs_16_.refs_8_, ...), custom_call_target="tpu_custom_call" | custom-call | flops 33554432 | bytes 25165824 | tf_op jit(solution)/shard_map/pallas_call | solution.py:179
  38.4 0.0 collective-permute-done.8.refs_13_
  38.4 10.5 %collective-permute-start.1 = (bf16[512,384]{1,0:T(8,128)(2,1)}, bf16[512,384]{1,0:T(8,128)(2,1)S(1)}, u32[]{:S(2)}, u32[]{:S(2)}) collective-permute-start(bf16[512,384]{1,0:T(8,128)(2,1)} %get-tuple-element.17), channel_id=1, source_target_pairs={{0,4},{1,5},{2,6},{3,7},{4,8},{5,9},{6,10},{7,11},{8,12},{9,13},{1... | collective-permute-start | bytes 1179656 | tf_op jit(solution)/shard_map/ppermute | solution.py:361
  48.9 0.0 collective-permute-done.5.refs_10_
  48.9 0.5 collective-permute-start.2
  49.4 1.5 %collective-permute-start.17 = (bf16[256,896]{1,0:T(8,128)(2,1)S(1)}, bf16[256,896]{1,0:T(8,128)(2,1)}, u32[]{:S(2)}, u32[]{:S(2)}) collective-permute-start(bf16[256,896]{1,0:T(8,128)(2,1)S(1)} %collective-permute-done.8.refs_13_), channel_id=1, source_target_pairs={{0,2},{1,3},{2,0},{3,1},{4,6},{5,7},{6,4},{7,5},{8,10},{9,11},{10,... | collective-permute-start | bytes 1376264 | tf_op jit(solution)/shard_map/ppermute | solution.py:361
  50.9 0.0 collective-permute-done.6.refs_11_
  50.9 1.5 %collective-permute-start.21 = (bf16[256,896]{1,0:T(8,128)(2,1)S(1)}, bf16[256,896]{1,0:T(8,128)(2,1)}, u32[]{:S(2)}, u32[]{:S(2)}) collective-permute-start(bf16[256,896]{1,0:T(8,128)(2,1)S(1)} %collective-permute-done.8.refs_13_), channel_id=1, source_target_pairs={{0,16},{16,0},{1,17},{17,1},{2,18},{18,2},{3,19},{19,3},{4,20},{20... | collective-permute-start | bytes 1376264 | tf_op jit(solution)/shard_map/ppermute | solution.py:353
  52.4 1.0 slice.7.refs_7_
  53.4 0.7 stack.94.place_ref
  54.1 0.5 collective-permute-start.19
  54.6 0.8 collective-permute-done.1.refs_14_.refs_9_.refs_8_
  55.4 1.5 %collective-permute-start.16 = (bf16[256,896]{1,0:T(8,128)(2,1)}, bf16[256,896]{1,0:T(8,128)(2,1)S(1)}, u32[]{:S(2)}, u32[]{:S(2)}) collective-permute-start(bf16[256,896]{1,0:T(8,128)(2,1)} %collective-permute-done.15.refs_4_), channel_id=1, source_target_pairs={{0,16},{16,0},{1,17},{17,1},{2,18},{18,2},{3,19},{19,3},{4,20},{20... | collective-permute-start | bytes 1376264 | tf_op jit(solution)/shard_map/ppermute | solution.py:353
  56.9 2.0 %collective-permute-done.2.refs_15_.refs_10_.refs_9_ = bf16[512,384]{1,0:T(8,128)(2,1)S(1)} collective-permute-done((bf16[512,384]{1,0:T(8,128)(2,1)}, bf16[512,384]{1,0:T(8,128)(2,1)S(1)}, u32[]{:S(2)}, u32[]{:S(2)}) %collective-permute-start.2) | collective-permute-done | bytes 393248 | tf_op jit(solution)/shard_map/ppermute | solution.py:361
  58.9 1.5 %collective-permute-start.22 = (bf16[256,896]{1,0:T(8,128)(2,1)}, bf16[256,896]{1,0:T(8,128)(2,1)S(1)}, u32[]{:S(2)}, u32[]{:S(2)}) collective-permute-start(bf16[256,896]{1,0:T(8,128)(2,1)} %collective-permute-done.5.refs_10_), channel_id=1, source_target_pairs={{0,16},{16,0},{1,17},{17,1},{2,18},{18,2},{3,19},{19,3},{4,20},{20... | collective-permute-start | bytes 1376264 | tf_op jit(solution)/shard_map/ppermute | solution.py:353
  60.4 10.2 %shard_map.83 = (f32[512,896]{1,0:T(8,128)}, f32[512,896]{1,0:T(8,128)}, bf16[512,384]{1,0:T(8,128)(2,1)}) custom-call(s32[7]{0:T(128)} %stack.94.place_ref, bf16[1024,4096]{1,0:T(8,128)(2,1)} %get-tuple-element.16.refs_0_.refs_1_.refs_2_.refs_3_.refs_4_.refs_5_.refs_6_.refs_7_, ...), custom_call_target="tpu_custom_call" | custom-call | flops 3758096384 | bytes 11534336 | tf_op jit(solution)/shard_map/pallas_call | solution.py:242
  70.7 2.9 %collective-permute-start.9 = (bf16[512,384]{1,0:T(8,128)(2,1)}, bf16[512,384]{1,0:T(8,128)(2,1)S(1)}, u32[]{:S(2)}, u32[]{:S(2)}) collective-permute-start(bf16[512,384]{1,0:T(8,128)(2,1)} %get-tuple-element.18), channel_id=1, source_target_pairs={{0,12},{1,13},{2,14},{3,15},{4,0},{5,1},{6,2},{7,3},{8,4},{9,5},{1... | collective-permute-start | bytes 1179656 | tf_op jit(solution)/shard_map/ppermute | solution.py:361
  73.6 0.0 collective-permute-start.11
  73.6 7.3 %collective-permute-done.22.refs_7_ = bf16[256,896]{1,0:T(8,128)(2,1)S(1)} collective-permute-done((bf16[256,896]{1,0:T(8,128)(2,1)}, bf16[256,896]{1,0:T(8,128)(2,1)S(1)}, u32[]{:S(2)}, u32[]{:S(2)}) %collective-permute-start.22) | collective-permute-done | bytes 458784 | tf_op jit(solution)/shard_map/ppermute | solution.py:353
  80.9 1.5 %collective-permute-start.18 = (bf16[256,896]{1,0:T(8,128)(2,1)}, bf16[256,896]{1,0:T(8,128)(2,1)S(1)}, u32[]{:S(2)}, u32[]{:S(2)}) collective-permute-start(bf16[256,896]{1,0:T(8,128)(2,1)} %collective-permute-done.17.refs_5_), channel_id=1, source_target_pairs={{0,16},{16,0},{1,17},{17,1},{2,18},{18,2},{3,19},{19,3},{4,20},{20... | collective-permute-start | bytes 1376264 | tf_op jit(solution)/shard_map/ppermute | solution.py:353
  82.4 0.0 collective-permute-done.19.refs_6_
  82.5 0.8 collective-permute-start.20
  83.2 0.0 collective-permute-done.16.refs_4_
  83.2 0.5 collective-permute-start.10
  83.8 1.5 %collective-permute-start.12 = (bf16[512,384]{1,0:T(8,128)(2,1)S(1)}, bf16[512,384]{1,0:T(8,128)(2,1)S(1)}, u32[]{:S(2)}, u32[]{:S(2)}) collective-permute-start(bf16[512,384]{1,0:T(8,128)(2,1)S(1)} %collective-permute-done.9.refs_11_), channel_id=1, source_target_pairs={{0,2},{1,3},{2,0},{3,1},{4,6},{5,7},{6,4},{7,5},{8,10},{9,11},{10,... | collective-permute-start | bytes 1179656 | tf_op jit(solution)/shard_map/ppermute | solution.py:361
  85.3 0.2 collective-permute-done.11.refs_13_.refs_12_
  85.5 0.5 collective-permute-start.13
  86.0 0.7 pad_add_fusion.1.place_ref
  86.7 0.7 pad_add_fusion.place_ref
  87.3 8.1 %shard_map.85 = (f32[512,896]{1,0:T(8,128)}, f32[512,896]{1,0:T(8,128)}) custom-call(s32[4]{0:T(128)} %pad_add_fusion.1.place_ref, bf16[1024,4096]{1,0:T(8,128)(2,1)} %get-tuple-element.16.refs_0_.refs_1_.refs_2_.refs_3_.refs_4_.refs_5_.refs_6_.refs_7_, ...), custom_call_target="tpu_custom_call", output_to_operand_aliasing={{0}: (9, {}), {1}: (10, {})} | custom-call | flops 1879048192 | bytes 11272192 | tf_op jit(solution)/shard_map/pallas_call | solution.py:242
  95.5 4.2 %collective-permute-done.13.refs_15_.refs_14_ = bf16[512,384]{1,0:T(8,128)(2,1)S(1)} collective-permute-done((bf16[512,384]{1,0:T(8,128)(2,1)S(1)}, bf16[512,384]{1,0:T(8,128)(2,1)S(1)}, u32[]{:S(2)}, u32[]{:S(2)}) %collective-permute-start.13) | collective-permute-done | bytes 393248 | tf_op jit(solution)/shard_map/ppermute | solution.py:361
  99.7 0.7 copy-done.15
  100.4 8.1 %shard_map.86 = (f32[512,896]{1,0:T(8,128)}, f32[512,896]{1,0:T(8,128)}) custom-call(s32[4]{0:T(128)} %pad_add_fusion.place_ref, bf16[1024,4096]{1,0:T(8,128)(2,1)} %get-tuple-element.16.refs_0_.refs_1_.refs_2_.refs_3_.refs_4_.refs_5_.refs_6_.refs_7_, ...), custom_call_target="tpu_custom_call", output_to_operand_aliasing={{0}: (16, {}), {1}: (17, {})} | custom-call | flops 1879048192 | bytes 11272192 | tf_op jit(solution)/shard_map/pallas_call | solution.py:242
  108.5 0.7 stack.87.place_ref
  109.2 0.0 copy-start.4
  109.2 0.0 copy-start.6
  109.2 10.4 %shard_map.84 = (f32[512,384]{1,0:T(8,128)}, f32[512,384]{1,0:T(8,128)}) custom-call(s32[8]{0:T(128)} %stack.87.place_ref, bf16[1024,4096]{1,0:T(8,128)(2,1)} %get-tuple-element.16.refs_0_.refs_1_.refs_2_.refs_3_.refs_4_.refs_5_.refs_6_.refs_7_, bf16[1024,4096]{1,0:T(8,128)(2,1)} %get-tuple-element.16.refs_0_.refs_1_.refs_2_.refs_3_.refs_4_.refs_5_.refs_6_.refs_7_, ...), custom_call_target="tpu_custom_call" | custom-call | flops 3221225472 | bytes 13107200 | tf_op jit(solution)/shard_map/pallas_call | solution.py:242
  119.6 0.6 collective-permute-start.14
  120.2 2.1 %collective-permute-done.14.got_b = f32[512,384]{1,0:T(8,128)S(1)} collective-permute-done((f32[512,384]{1,0:T(8,128)}, f32[512,384]{1,0:T(8,128)S(1)}, u32[]{:S(2)}, u32[]{:S(2)}) %collective-permute-start.14) | collective-permute-done | bytes 786464 | tf_op jit(solution)/shard_map/ppermute | solution.py:361
  122.3 0.0 copy-start.5
  122.4 1.1 copy-done.5
  123.5 15.1 %shard_map.87 = bf16[512,1024]{1,0:T(8,128)(2,1)} custom-call(s32[2]{0:T(128)S(1)} %copy-done.6, s32[2]{0:T(128)S(1)} %copy-done.7, f32[512,384]{1,0:T(8,128)S(1)} %copy-done.5, f32[512,384]{1,0:T(8,128)S(1)} %collective-permute-done.14.got_b, f32[512,896]{1,0:T(8,128)S(1)} %copy-done, f32[512,896]{1,0:T(8,128)} %collective-permute-done.23.got_a, ...), custom_call_target="tpu_custom_call" | custom-call | flops 2684354560 | bytes 20971520 | tf_op jit(solution)/shard_map/pallas_call | solution.py:312
  (53 shorter events, 0.1 us)
Async XLA Ops:
  0.0 22.4 %collective-permute-start = (bf16[512,8192]{1,0:T(8,128)(2,1)}, bf16[512,8192]{1,0:T(8,128)(2,1)}, u32[]{:S(2)}, u32[]{:S(2)}) collective-permute-start(bf16[512,8192]{1,0:T(8,128)(2,1)} %x_ref.1), channel_id=1, source_target_pairs={{0,1},{1,0},{2,3},{3,2},{4,5},{5,4},{6,7},{7,6},{8,9},{9,8},{10,11... | collective-permute-start | bytes 25165832 | tf_op jit(solution)/shard_map/ppermute | solution.py:361
  1.5 16.2 %collective-permute-start.4 = (bf16[256,896]{1,0:T(8,128)(2,1)S(1)}, bf16[256,896]{1,0:T(8,128)(2,1)}, u32[]{:S(2)}, u32[]{:S(2)}) collective-permute-start(bf16[256,896]{1,0:T(8,128)(2,1)S(1)} %constant_dynamic-slice_fusion), channel_id=1, source_target_pairs={{0,4},{1,5},{2,6},{3,7},{4,8},{5,9},{6,10},{7,11},{8,12},{9,13},{1... | collective-permute-start | bytes 1376264 | tf_op jit(solution)/shard_map/ppermute | solution.py:361
  4.1 34.2 %collective-permute-start.8 = (bf16[256,896]{1,0:T(8,128)(2,1)S(1)}, bf16[256,896]{1,0:T(8,128)(2,1)S(1)}, u32[]{:S(2)}, u32[]{:S(2)}) collective-permute-start(bf16[256,896]{1,0:T(8,128)(2,1)S(1)} %constant_dynamic-slice_fusion), channel_id=1, source_target_pairs={{0,12},{1,13},{2,14},{3,15},{4,0},{5,1},{6,2},{7,3},{8,4},{9,5},{1... | collective-permute-start | bytes 1376264 | tf_op jit(solution)/shard_map/ppermute | solution.py:361
  6.2 14.6 %collective-permute-start.3 = (bf16[256,896]{1,0:T(8,128)(2,1)S(1)}, bf16[256,896]{1,0:T(8,128)(2,1)}, u32[]{:S(2)}, u32[]{:S(2)}) collective-permute-start(bf16[256,896]{1,0:T(8,128)(2,1)S(1)} %constant_dynamic-slice_fusion), channel_id=1, source_target_pairs={{0,2},{1,3},{2,0},{3,1},{4,6},{5,7},{6,4},{7,5},{8,10},{9,11},{10,... | collective-permute-start | bytes 1376264 | tf_op jit(solution)/shard_map/ppermute | solution.py:361
  9.6 2.3 %copy-start.7 = (s32[2]{0:T(128)S(1)}, s32[2]{0:T(128)}, u32[]{:S(2)}) copy-start(s32[2]{0:T(128)} %len_ref.1) | copy-start | bytes 28
  10.7 12.8 %copy-start.10 = (bf16[512,1280]{1,0:T(8,128)(2,1)S(1)}, bf16[512,1280]{1,0:T(8,128)(2,1)}, u32[]{:S(2)}) copy-start(bf16[512,1280]{1,0:T(8,128)(2,1)} %param.14) | copy-start | bytes 3932164
  17.7 31.2 %collective-permute-start.5 = (bf16[256,896]{1,0:T(8,128)(2,1)}, bf16[256,896]{1,0:T(8,128)(2,1)}, u32[]{:S(2)}, u32[]{:S(2)}) collective-permute-start(bf16[256,896]{1,0:T(8,128)(2,1)} %collective-permute-done.4.refs_9_), channel_id=1, source_target_pairs={{0,2},{1,3},{2,0},{3,1},{4,6},{5,7},{6,4},{7,5},{8,10},{9,11},{10,... | collective-permute-start | bytes 1376264 | tf_op jit(solution)/shard_map/ppermute | solution.py:361
  19.3 30.1 %collective-permute-start.7 = (bf16[256,896]{1,0:T(8,128)(2,1)}, bf16[256,896]{1,0:T(8,128)(2,1)}, u32[]{:S(2)}, u32[]{:S(2)}) collective-permute-start(bf16[256,896]{1,0:T(8,128)(2,1)} %collective-permute-done.4.refs_9_), channel_id=1, source_target_pairs={{0,16},{16,0},{1,17},{17,1},{2,18},{18,2},{3,19},{19,3},{4,20},{20... | collective-permute-start | bytes 1376264 | tf_op jit(solution)/shard_map/ppermute | solution.py:353
  20.8 30.0 %collective-permute-start.6 = (bf16[256,896]{1,0:T(8,128)(2,1)}, bf16[256,896]{1,0:T(8,128)(2,1)}, u32[]{:S(2)}, u32[]{:S(2)}) collective-permute-start(bf16[256,896]{1,0:T(8,128)(2,1)} %collective-permute-done.3.refs_8_), channel_id=1, source_target_pairs={{0,16},{16,0},{1,17},{17,1},{2,18},{18,2},{3,19},{19,3},{4,20},{20... | collective-permute-start | bytes 1376264 | tf_op jit(solution)/shard_map/ppermute | solution.py:353
  22.4 31.7 %collective-permute-start.15 = (bf16[256,896]{1,0:T(8,128)(2,1)}, bf16[256,896]{1,0:T(8,128)(2,1)}, u32[]{:S(2)}, u32[]{:S(2)}) collective-permute-start(bf16[256,896]{1,0:T(8,128)(2,1)} %collective-permute-done.4.refs_9_), channel_id=1, source_target_pairs={{0,4},{1,5},{2,6},{3,7},{4,8},{5,9},{6,10},{7,11},{8,12},{9,13},{1... | collective-permute-start | bytes 1376264 | tf_op jit(solution)/shard_map/ppermute | solution.py:361
  38.4 22.1 %copy-start.16 = (bf16[256,896]{1,0:T(8,128)(2,1)}, bf16[256,896]{1,0:T(8,128)(2,1)S(1)}, u32[]{:S(2)}) copy-start(bf16[256,896]{1,0:T(8,128)(2,1)S(1)} %collective-permute-done.8.refs_13_) | copy-start | bytes 1376260
  38.4 17.0 %collective-permute-start.1 = (bf16[512,384]{1,0:T(8,128)(2,1)}, bf16[512,384]{1,0:T(8,128)(2,1)S(1)}, u32[]{:S(2)}, u32[]{:S(2)}) collective-permute-start(bf16[512,384]{1,0:T(8,128)(2,1)} %get-tuple-element.17), channel_id=1, source_target_pairs={{0,4},{1,5},{2,6},{3,7},{4,8},{5,9},{6,10},{7,11},{8,12},{9,13},{1... | collective-permute-start | bytes 1179656 | tf_op jit(solution)/shard_map/ppermute | solution.py:361
  48.9 10.1 %collective-permute-start.2 = (bf16[512,384]{1,0:T(8,128)(2,1)}, bf16[512,384]{1,0:T(8,128)(2,1)S(1)}, u32[]{:S(2)}, u32[]{:S(2)}) collective-permute-start(bf16[512,384]{1,0:T(8,128)(2,1)} %get-tuple-element.17), channel_id=1, source_target_pairs={{0,2},{1,3},{2,0},{3,1},{4,6},{5,7},{6,4},{7,5},{8,10},{9,11},{10,... | collective-permute-start | bytes 1179656 | tf_op jit(solution)/shard_map/ppermute | solution.py:361
  49.4 21.3 %collective-permute-start.17 = (bf16[256,896]{1,0:T(8,128)(2,1)S(1)}, bf16[256,896]{1,0:T(8,128)(2,1)}, u32[]{:S(2)}, u32[]{:S(2)}) collective-permute-start(bf16[256,896]{1,0:T(8,128)(2,1)S(1)} %collective-permute-done.8.refs_13_), channel_id=1, source_target_pairs={{0,2},{1,3},{2,0},{3,1},{4,6},{5,7},{6,4},{7,5},{8,10},{9,11},{10,... | collective-permute-start | bytes 1376264 | tf_op jit(solution)/shard_map/ppermute | solution.py:361
  50.9 22.7 %collective-permute-start.21 = (bf16[256,896]{1,0:T(8,128)(2,1)S(1)}, bf16[256,896]{1,0:T(8,128)(2,1)}, u32[]{:S(2)}, u32[]{:S(2)}) collective-permute-start(bf16[256,896]{1,0:T(8,128)(2,1)S(1)} %collective-permute-done.8.refs_13_), channel_id=1, source_target_pairs={{0,16},{16,0},{1,17},{17,1},{2,18},{18,2},{3,19},{19,3},{4,20},{20... | collective-permute-start | bytes 1376264 | tf_op jit(solution)/shard_map/ppermute | solution.py:353
  54.1 28.4 %collective-permute-start.19 = (bf16[256,896]{1,0:T(8,128)(2,1)}, bf16[256,896]{1,0:T(8,128)(2,1)S(1)}, u32[]{:S(2)}, u32[]{:S(2)}) collective-permute-start(bf16[256,896]{1,0:T(8,128)(2,1)} %collective-permute-done.15.refs_4_), channel_id=1, source_target_pairs={{0,2},{1,3},{2,0},{3,1},{4,6},{5,7},{6,4},{7,5},{8,10},{9,11},{10,... | collective-permute-start | bytes 1376264 | tf_op jit(solution)/shard_map/ppermute | solution.py:361
  55.4 5.0 %copy-start.8 = (bf16[512,384]{1,0:T(8,128)(2,1)}, bf16[512,384]{1,0:T(8,128)(2,1)S(1)}, u32[]{:S(2)}) copy-start(bf16[512,384]{1,0:T(8,128)(2,1)S(1)} %collective-permute-done.1.refs_14_.refs_9_.refs_8_) | copy-start | bytes 1179652
  55.4 27.8 %collective-permute-start.16 = (bf16[256,896]{1,0:T(8,128)(2,1)}, bf16[256,896]{1,0:T(8,128)(2,1)S(1)}, u32[]{:S(2)}, u32[]{:S(2)}) collective-permute-start(bf16[256,896]{1,0:T(8,128)(2,1)} %collective-permute-done.15.refs_4_), channel_id=1, source_target_pairs={{0,16},{16,0},{1,17},{17,1},{2,18},{18,2},{3,19},{19,3},{4,20},{20... | collective-permute-start | bytes 1376264 | tf_op jit(solution)/shard_map/ppermute | solution.py:353
  58.9 1.5 %copy-start.9 = (bf16[512,384]{1,0:T(8,128)(2,1)}, bf16[512,384]{1,0:T(8,128)(2,1)S(1)}, u32[]{:S(2)}) copy-start(bf16[512,384]{1,0:T(8,128)(2,1)S(1)} %collective-permute-done.2.refs_15_.refs_10_.refs_9_) | copy-start | bytes 1179652
  58.9 22.0 %collective-permute-start.22 = (bf16[256,896]{1,0:T(8,128)(2,1)}, bf16[256,896]{1,0:T(8,128)(2,1)S(1)}, u32[]{:S(2)}, u32[]{:S(2)}) collective-permute-start(bf16[256,896]{1,0:T(8,128)(2,1)} %collective-permute-done.5.refs_10_), channel_id=1, source_target_pairs={{0,16},{16,0},{1,17},{17,1},{2,18},{18,2},{3,19},{19,3},{4,20},{20... | collective-permute-start | bytes 1376264 | tf_op jit(solution)/shard_map/ppermute | solution.py:353
  70.7 13.1 %collective-permute-start.9 = (bf16[512,384]{1,0:T(8,128)(2,1)}, bf16[512,384]{1,0:T(8,128)(2,1)S(1)}, u32[]{:S(2)}, u32[]{:S(2)}) collective-permute-start(bf16[512,384]{1,0:T(8,128)(2,1)} %get-tuple-element.18), channel_id=1, source_target_pairs={{0,12},{1,13},{2,14},{3,15},{4,0},{5,1},{6,2},{7,3},{8,4},{9,5},{1... | collective-permute-start | bytes 1179656 | tf_op jit(solution)/shard_map/ppermute | solution.py:361
  73.6 11.9 %collective-permute-start.11 = (bf16[512,384]{1,0:T(8,128)(2,1)}, bf16[512,384]{1,0:T(8,128)(2,1)S(1)}, u32[]{:S(2)}, u32[]{:S(2)}) collective-permute-start(bf16[512,384]{1,0:T(8,128)(2,1)} %copy-done.8), channel_id=1, source_target_pairs={{0,4},{1,5},{2,6},{3,7},{4,8},{5,9},{6,10},{7,11},{8,12},{9,13},{1... | collective-permute-start | bytes 1179656 | tf_op jit(solution)/shard_map/ppermute | solution.py:361
  80.9 1.5 %copy-start.20 = (bf16[256,896]{1,0:T(8,128)(2,1)}, bf16[256,896]{1,0:T(8,128)(2,1)S(1)}, u32[]{:S(2)}) copy-start(bf16[256,896]{1,0:T(8,128)(2,1)S(1)} %collective-permute-done.22.refs_7_) | copy-start | bytes 1376260
  80.9 14.5 %collective-permute-start.18 = (bf16[256,896]{1,0:T(8,128)(2,1)}, bf16[256,896]{1,0:T(8,128)(2,1)S(1)}, u32[]{:S(2)}, u32[]{:S(2)}) collective-permute-start(bf16[256,896]{1,0:T(8,128)(2,1)} %collective-permute-done.17.refs_5_), channel_id=1, source_target_pairs={{0,16},{16,0},{1,17},{17,1},{2,18},{18,2},{3,19},{19,3},{4,20},{20... | collective-permute-start | bytes 1376264 | tf_op jit(solution)/shard_map/ppermute | solution.py:353
  82.4 13.0 %copy-start.17 = (bf16[256,896]{1,0:T(8,128)(2,1)}, bf16[256,896]{1,0:T(8,128)(2,1)S(1)}, u32[]{:S(2)}) copy-start(bf16[256,896]{1,0:T(8,128)(2,1)S(1)} %collective-permute-done.19.refs_6_) | copy-start | bytes 1376260
  82.5 13.0 %collective-permute-start.20 = (bf16[256,896]{1,0:T(8,128)(2,1)S(1)}, bf16[256,896]{1,0:T(8,128)(2,1)}, u32[]{:S(2)}, u32[]{:S(2)}) collective-permute-start(bf16[256,896]{1,0:T(8,128)(2,1)S(1)} %collective-permute-done.19.refs_6_), channel_id=1, source_target_pairs={{0,16},{16,0},{1,17},{17,1},{2,18},{18,2},{3,19},{19,3},{4,20},{20... | collective-permute-start | bytes 1376264 | tf_op jit(solution)/shard_map/ppermute | solution.py:353
  83.2 12.2 %copy-start.18 = (bf16[256,896]{1,0:T(8,128)(2,1)}, bf16[256,896]{1,0:T(8,128)(2,1)S(1)}, u32[]{:S(2)}) copy-start(bf16[256,896]{1,0:T(8,128)(2,1)S(1)} %collective-permute-done.16.refs_4_) | copy-start | bytes 1376260
  83.2 12.2 %collective-permute-start.10 = (bf16[512,384]{1,0:T(8,128)(2,1)}, bf16[512,384]{1,0:T(8,128)(2,1)S(1)}, u32[]{:S(2)}, u32[]{:S(2)}) collective-permute-start(bf16[512,384]{1,0:T(8,128)(2,1)} %copy-done.8), channel_id=1, source_target_pairs={{0,2},{1,3},{2,0},{3,1},{4,6},{5,7},{6,4},{7,5},{8,10},{9,11},{10,... | collective-permute-start | bytes 1179656 | tf_op jit(solution)/shard_map/ppermute | solution.py:361
  83.8 11.6 %copy-start.11 = (bf16[512,384]{1,0:T(8,128)(2,1)}, bf16[512,384]{1,0:T(8,128)(2,1)S(1)}, u32[]{:S(2)}) copy-start(bf16[512,384]{1,0:T(8,128)(2,1)S(1)} %collective-permute-done.9.refs_11_) | copy-start | bytes 1179652
  83.8 11.7 %collective-permute-start.12 = (bf16[512,384]{1,0:T(8,128)(2,1)S(1)}, bf16[512,384]{1,0:T(8,128)(2,1)S(1)}, u32[]{:S(2)}, u32[]{:S(2)}) collective-permute-start(bf16[512,384]{1,0:T(8,128)(2,1)S(1)} %collective-permute-done.9.refs_11_), channel_id=1, source_target_pairs={{0,2},{1,3},{2,0},{3,1},{4,6},{5,7},{6,4},{7,5},{8,10},{9,11},{10,... | collective-permute-start | bytes 1179656 | tf_op jit(solution)/shard_map/ppermute | solution.py:361
  85.5 10.0 %copy-start.12 = (bf16[512,384]{1,0:T(8,128)(2,1)}, bf16[512,384]{1,0:T(8,128)(2,1)S(1)}, u32[]{:S(2)}) copy-start(bf16[512,384]{1,0:T(8,128)(2,1)S(1)} %collective-permute-done.11.refs_13_.refs_12_) | copy-start | bytes 1179652
  85.5 14.2 %collective-permute-start.13 = (bf16[512,384]{1,0:T(8,128)(2,1)S(1)}, bf16[512,384]{1,0:T(8,128)(2,1)S(1)}, u32[]{:S(2)}, u32[]{:S(2)}) collective-permute-start(bf16[512,384]{1,0:T(8,128)(2,1)S(1)} %collective-permute-done.11.refs_13_.refs_12_), channel_id=1, source_target_pairs={{0,2},{1,3},{2,0},{3,1},{4,6},{5,7},{6,4},{7,5},{8,10},{9,11},{10,... | collective-permute-start | bytes 1179656 | tf_op jit(solution)/shard_map/ppermute | solution.py:361
  95.4 4.2 %copy-start.19 = (bf16[256,896]{1,0:T(8,128)(2,1)}, bf16[256,896]{1,0:T(8,128)(2,1)S(1)}, u32[]{:S(2)}) copy-start(bf16[256,896]{1,0:T(8,128)(2,1)S(1)} %collective-permute-done.18.refs_5_) | copy-start | bytes 1376260
  95.5 4.2 %copy-start.13 = (bf16[512,384]{1,0:T(8,128)(2,1)}, bf16[512,384]{1,0:T(8,128)(2,1)S(1)}, u32[]{:S(2)}) copy-start(bf16[512,384]{1,0:T(8,128)(2,1)S(1)} %collective-permute-done.10.refs_12_.refs_10_) | copy-start | bytes 1179652
  95.5 4.2 %copy-start.14 = (bf16[512,384]{1,0:T(8,128)(2,1)}, bf16[512,384]{1,0:T(8,128)(2,1)S(1)}, u32[]{:S(2)}) copy-start(bf16[512,384]{1,0:T(8,128)(2,1)S(1)} %collective-permute-done.12.refs_14_.refs_13_) | copy-start | bytes 1179652
  99.7 0.7 copy-start.15
  108.5 13.8 %collective-permute-start.23 = (f32[512,896]{1,0:T(8,128)}, f32[512,896]{1,0:T(8,128)}, u32[]{:S(2)}, u32[]{:S(2)}) collective-permute-start(f32[512,896]{1,0:T(8,128)} %get-tuple-element.26), channel_id=1, source_target_pairs={{0,1},{1,0},{2,3},{3,2},{4,5},{5,4},{6,7},{7,6},{8,9},{9,8},{10,11... | collective-permute-start | bytes 5505032 | tf_op jit(solution)/shard_map/ppermute | solution.py:361
  109.2 11.0 %copy-start.21 = (f32[1280]{0:T(1024)S(1)}, f32[1280]{0:T(1024)}, u32[]{:S(2)}) copy-start(f32[1280]{0:T(1024)} %param.15) | copy-start | bytes 15364
  109.2 13.1 %copy-start = (f32[512,896]{1,0:T(8,128)S(1)}, f32[512,896]{1,0:T(8,128)}, u32[]{:S(2)}) copy-start(f32[512,896]{1,0:T(8,128)} %get-tuple-element.25.own_a) | copy-start | bytes 5505028
  109.2 13.1 %copy-start.1 = (f32[2,256,128]{2,1,0:T(8,128)S(1)}, f32[2,256,128]{2,1,0:T(8,128)}, u32[]{:S(2)}) copy-start(f32[2,256,128]{2,1,0:T(8,128)} %get-tuple-element.32.refs_1_.cos_ref) | copy-start | bytes 786436
  109.2 13.1 %copy-start.2 = (f32[2,256,128]{2,1,0:T(8,128)S(1)}, f32[2,256,128]{2,1,0:T(8,128)}, u32[]{:S(2)}) copy-start(f32[2,256,128]{2,1,0:T(8,128)} %get-tuple-element.33.refs_2_.sin_ref) | copy-start | bytes 786436
  109.2 13.1 %copy-start.3 = (f32[2,256,256]{2,1,0:T(8,128)S(1)}, f32[2,256,256]{2,1,0:T(8,128)}, u32[]{:S(2)}) copy-start(f32[2,256,256]{2,1,0:T(8,128)} %get-tuple-element.28.refs_0_.bias_ref) | copy-start | bytes 1572868
  109.2 13.1 %copy-start.4 = (bf16[2,2,1024,128]{3,2,1,0:T(8,128)(2,1)S(1)}, bf16[2,2,1024,128]{3,2,1,0:T(8,128)(2,1)}, u32[]{:S(2)}) copy-start(bf16[2,2,1024,128]{3,2,1,0:T(8,128)(2,1)} %cache_ref.1) | copy-start | bytes 3145732
  109.2 13.1 %copy-start.6 = (s32[2]{0:T(128)S(1)}, s32[2]{0:T(128)}, u32[]{:S(2)}) copy-start(s32[2]{0:T(128)} %kept_ref.1) | copy-start | bytes 28
  119.6 2.7 %collective-permute-start.14 = (f32[512,384]{1,0:T(8,128)}, f32[512,384]{1,0:T(8,128)S(1)}, u32[]{:S(2)}, u32[]{:S(2)}) collective-permute-start(f32[512,384]{1,0:T(8,128)} %get-tuple-element.20), channel_id=1, source_target_pairs={{0,1},{1,0},{2,3},{3,2},{4,5},{5,4},{6,7},{7,6},{8,9},{9,8},{10,11... | collective-permute-start | bytes 2359304 | tf_op jit(solution)/shard_map/ppermute | solution.py:361
  122.3 1.1 copy-start.5

commit v4 on v3

--- a/solution.py
+++ b/solution.py
@@ -345,7 +345,7 @@
     "a y z2 yz2", "a x z2 x2", "a y x3 yx3", "b x z2 x2", "a y x2 yx2",
     MIDDLE, LAST, ("b", ("own", "z1", "x0", "z3", "x1", "z2", "x3", "x2")),
 )
-WAITED = {GATE: ("z1", "x0"), LAST: ("z1", "x0", "x1", "z3", "z2", "x3", "x2")}
+WAITED = {GATE: ("z1", "x0"), MIDDLE: ("z3", "x1"), LAST: ("z1", "x0", "x1", "z3", "z2", "x3", "x2")}
 
 
 def move(array, way):

time: 139 us -> 136 us (0.978)
  waiting for transfers between devices: 22.2 us -> 19.5 us
    ppermute x7, waiting for transfers between devices: 7.33 us -> 0.02 us  [move(): return lax.ppermute(array, 'groups', [(0, 1), (1, 0)])]
    ppermute x17, waiting for transfers between devices: 14.9 us -> 19.4 us  [move(): return lax.ppermute(array, 'dp', pairs)]
  transfers between devices with their start and end apart: 24 -> 24, of which waited for: 7 -> 7; matrix products, arithmetic and copies ran while one was open for 8% -> 9% of each run, Pallas kernels for 31% -> 31%
where the time goes in v4:
time: 136 us
  Pallas kernels  65.8 us (48%)
  starting transfers between devices  35.4 us (26%)
  waiting for transfers between devices  19.5 us (14%)
  local copies, waits for them, and re-layouts  6.87 us (5%)
  other arithmetic  4.04 us (3%)
  matrix products  3.99 us (3%)
    pallas_call x4, Pallas kernels, accumulate(): pl.pallas_call(functools.partial(accumulate_kernel, count, len(unread), f...  36.7 us
    ppermute x17, starting transfers between devices, move(): return lax.ppermute(array, 'dp', pairs)  27.6 us
    ppermute x17, waiting for transfers between devices, move(): return lax.ppermute(array, 'dp', pairs)  19.4 us
    pallas_call x1, Pallas kernels, attend_sums(): pl.pallas_call(heads_kernel, out_shape=jax.ShapeDtypeStruct((rows, GROUP...  15.1 us
    pallas_call x1, Pallas kernels, normalize_both(): pl.pallas_call(functools.partial(norm_kernel, steps), out_shape=(jax.Shap...  14 us
    ppermute x7, starting transfers between devices, move(): return lax.ppermute(array, 'groups', [(0, 1), (1, 0)])  7.79 us
    dot_general x4, matrix products, tree_tables(): jnp.einsum('rij,rjk->rik', reached, reached, preferred_element_type=jnp.f...  3.99 us
  transfers between devices with their start and end apart: 24, of which 7 were waited for; matrix products, arithmetic and copies ran while one was open for 9% of the time, Pallas kernels for 31%

profile of v4, /device:TPU:0, one launch (start us, length us, event | category | flops | bytes accessed | tf_op | source)
XLA Modules:
  0.0 135.9 jit_solution(17590690774878934990)
XLA Ops:
  0.0 0.5 collective-permute-start
  0.5 1.1 constant_dynamic-slice_fusion
  1.5 2.6 %collective-permute-start.4 = (bf16[256,896]{1,0:T(8,128)(2,1)S(1)}, bf16[256,896]{1,0:T(8,128)(2,1)}, u32[]{:S(2)}, u32[]{:S(2)}) collective-permute-start(bf16[256,896]{1,0:T(8,128)(2,1)S(1)} %constant_dynamic-slice_fusion), channel_id=1, source_target_pairs={{0,4},{1,5},{2,6},{3,7},{4,8},{5,9},{6,10},{7,11},{8,12},{9,13},{1... | collective-permute-start | bytes 1376264 | tf_op jit(solution)/shard_map/ppermute | solution.py:361
  4.1 2.1 %collective-permute-start.8 = (bf16[256,896]{1,0:T(8,128)(2,1)S(1)}, bf16[256,896]{1,0:T(8,128)(2,1)S(1)}, u32[]{:S(2)}, u32[]{:S(2)}) collective-permute-start(bf16[256,896]{1,0:T(8,128)(2,1)S(1)} %constant_dynamic-slice_fusion), channel_id=1, source_target_pairs={{0,12},{1,13},{2,14},{3,15},{4,0},{5,1},{6,2},{7,3},{8,4},{9,5},{1... | collective-permute-start | bytes 1376264 | tf_op jit(solution)/shard_map/ppermute | solution.py:361
  6.2 1.6 %collective-permute-start.3 = (bf16[256,896]{1,0:T(8,128)(2,1)S(1)}, bf16[256,896]{1,0:T(8,128)(2,1)}, u32[]{:S(2)}, u32[]{:S(2)}) collective-permute-start(bf16[256,896]{1,0:T(8,128)(2,1)S(1)} %constant_dynamic-slice_fusion), channel_id=1, source_target_pairs={{0,2},{1,3},{2,0},{3,1},{4,6},{5,7},{6,4},{7,5},{8,10},{9,11},{10,... | collective-permute-start | bytes 1376264 | tf_op jit(solution)/shard_map/ppermute | solution.py:361
  7.9 0.7 convert_element_type.39
  8.6 1.7 %fusion.1 = bf16[2,256,256]{2,1,0:T(8,128)(2,1)S(1)} fusion(s32[2,256]{1,0:T(2,128)} %param.10, pred[256]{0:T(512)(128)(4,1)S(1)} %iota_compare_fusion.2, pred[256,256]{1,0:T(8,128)(4,1)S(1)} %iota_compare_fusion.1), kind=kOutput, calls=%fused_computation.9 | convolution fusion | flops 135135232 | bytes 329984 | tf_op jit(solution)/shard_map/rij,rjk->rik/dot_general | solution.py:31
  10.3 0.5 fusion.3
  10.8 0.5 fusion.5
  11.3 0.0 copy-start.12
  11.3 1.3 convert_reduce_fusion
  12.6 0.1 add_add_fusion
  12.7 5.0 %collective-permute-done.4.refs_9_ = bf16[256,896]{1,0:T(8,128)(2,1)} collective-permute-done((bf16[256,896]{1,0:T(8,128)(2,1)S(1)}, bf16[256,896]{1,0:T(8,128)(2,1)}, u32[]{:S(2)}, u32[]{:S(2)}) %collective-permute-start.4) | collective-permute-done | bytes 458784 | tf_op jit(solution)/shard_map/ppermute | solution.py:361
  17.7 1.6 %collective-permute-start.5 = (bf16[256,896]{1,0:T(8,128)(2,1)}, bf16[256,896]{1,0:T(8,128)(2,1)}, u32[]{:S(2)}, u32[]{:S(2)}) collective-permute-start(bf16[256,896]{1,0:T(8,128)(2,1)} %collective-permute-done.4.refs_9_), channel_id=1, source_target_pairs={{0,2},{1,3},{2,0},{3,1},{4,6},{5,7},{6,4},{7,5},{8,10},{9,11},{10,... | collective-permute-start | bytes 1376264 | tf_op jit(solution)/shard_map/ppermute | solution.py:361
  19.3 1.0 fusion.22
  20.3 1.6 %collective-permute-start.7 = (bf16[256,896]{1,0:T(8,128)(2,1)}, bf16[256,896]{1,0:T(8,128)(2,1)}, u32[]{:S(2)}, u32[]{:S(2)}) collective-permute-start(bf16[256,896]{1,0:T(8,128)(2,1)} %collective-permute-done.4.refs_9_), channel_id=1, source_target_pairs={{0,16},{16,0},{1,17},{17,1},{2,18},{18,2},{3,19},{19,3},{4,20},{20... | collective-permute-start | bytes 1376264 | tf_op jit(solution)/shard_map/ppermute | solution.py:353
  21.9 0.6 collective-permute-start.6
  22.5 1.0 pad_maximum_fusion
  23.5 0.8 slice.6.w_ref.refs_16_.refs_8_
  24.3 14.0 %shard_map.82 = (bf16[1024,4096]{1,0:T(8,128)(2,1)}, bf16[512,384]{1,0:T(8,128)(2,1)}) custom-call(s32[1]{0:T(128)} %bitcast.8.core_ref, bf16[512,8192]{1,0:T(8,128)(2,1)} %x_ref.1, bf16[512,8192]{1,0:T(8,128)(2,1)} %collective-permute-done.other_ref, f32[1,8192]{1,0:T(1,128)} %bitcast.30, bf16[512,384]{1,0:T(8,128)(2,1)} %slice.6.w_ref.refs_16_.refs_8_, ...), custom_call_target="tpu_custom_call" | custom-call | flops 33554432 | bytes 25165824 | tf_op jit(solution)/shard_map/pallas_call | solution.py:179
  38.3 0.0 collective-permute-done.8.refs_13_
  38.3 10.4 %collective-permute-start.1 = (bf16[512,384]{1,0:T(8,128)(2,1)}, bf16[512,384]{1,0:T(8,128)(2,1)S(1)}, u32[]{:S(2)}, u32[]{:S(2)}) collective-permute-start(bf16[512,384]{1,0:T(8,128)(2,1)} %get-tuple-element.17), channel_id=1, source_target_pairs={{0,4},{1,5},{2,6},{3,7},{4,8},{5,9},{6,10},{7,11},{8,12},{9,13},{1... | collective-permute-start | bytes 1179656 | tf_op jit(solution)/shard_map/ppermute | solution.py:361
  48.7 0.5 collective-permute-start.2
  49.3 0.0 collective-permute-done.7.refs_12_
  49.3 1.5 %collective-permute-start.17 = (bf16[256,896]{1,0:T(8,128)(2,1)S(1)}, bf16[256,896]{1,0:T(8,128)(2,1)S(1)}, u32[]{:S(2)}, u32[]{:S(2)}) collective-permute-start(bf16[256,896]{1,0:T(8,128)(2,1)S(1)} %collective-permute-done.8.refs_13_), channel_id=1, source_target_pairs={{0,2},{1,3},{2,0},{3,1},{4,6},{5,7},{6,4},{7,5},{8,10},{9,11},{10,... | collective-permute-start | bytes 1376264 | tf_op jit(solution)/shard_map/ppermute | solution.py:361
  50.8 1.5 %collective-permute-start.21 = (bf16[256,896]{1,0:T(8,128)(2,1)S(1)}, bf16[256,896]{1,0:T(8,128)(2,1)}, u32[]{:S(2)}, u32[]{:S(2)}) collective-permute-start(bf16[256,896]{1,0:T(8,128)(2,1)S(1)} %collective-permute-done.8.refs_13_), channel_id=1, source_target_pairs={{0,16},{16,0},{1,17},{17,1},{2,18},{18,2},{3,19},{19,3},{4,20},{20... | collective-permute-start | bytes 1376264 | tf_op jit(solution)/shard_map/ppermute | solution.py:353
  52.3 1.0 slice.7.refs_7_
  53.3 0.7 stack.94.place_ref
  53.9 0.5 collective-permute-start.22
  54.4 0.9 collective-permute-done.1.refs_14_.refs_9_.refs_8_
  55.3 0.5 collective-permute-start.19
  55.9 2.9 %collective-permute-done.2.refs_15_.refs_10_.refs_9_ = bf16[512,384]{1,0:T(8,128)(2,1)S(1)} collective-permute-done((bf16[512,384]{1,0:T(8,128)(2,1)}, bf16[512,384]{1,0:T(8,128)(2,1)S(1)}, u32[]{:S(2)}, u32[]{:S(2)}) %collective-permute-start.2) | collective-permute-done | bytes 393248 | tf_op jit(solution)/shard_map/ppermute | solution.py:361
  58.8 0.7 copy-done.9
  59.5 10.2 %shard_map.83 = (f32[512,896]{1,0:T(8,128)}, f32[512,896]{1,0:T(8,128)}, bf16[512,384]{1,0:T(8,128)(2,1)}) custom-call(s32[7]{0:T(128)} %stack.94.place_ref, bf16[1024,4096]{1,0:T(8,128)(2,1)} %get-tuple-element.16.refs_0_.refs_1_.refs_2_.refs_3_.refs_4_.refs_5_.refs_6_.refs_7_, ...), custom_call_target="tpu_custom_call" | custom-call | flops 3758096384 | bytes 11534336 | tf_op jit(solution)/shard_map/pallas_call | solution.py:242
  69.7 3.0 %collective-permute-start.9 = (bf16[512,384]{1,0:T(8,128)(2,1)}, bf16[512,384]{1,0:T(8,128)(2,1)S(1)}, u32[]{:S(2)}, u32[]{:S(2)}) collective-permute-start(bf16[512,384]{1,0:T(8,128)(2,1)} %get-tuple-element.18), channel_id=1, source_target_pairs={{0,12},{1,13},{2,14},{3,15},{4,0},{5,1},{6,2},{7,3},{8,4},{9,5},{1... | collective-permute-start | bytes 1179656 | tf_op jit(solution)/shard_map/ppermute | solution.py:361
  72.7 0.6 collective-permute-start.10
  73.3 0.0 collective-permute-start.11
  73.3 1.6 %collective-permute-start.16 = (bf16[256,896]{1,0:T(8,128)(2,1)S(1)}, bf16[256,896]{1,0:T(8,128)(2,1)S(1)}, u32[]{:S(2)}, u32[]{:S(2)}) collective-permute-start(bf16[256,896]{1,0:T(8,128)(2,1)S(1)} %collective-permute-done.15.refs_4_), channel_id=1, source_target_pairs={{0,16},{16,0},{1,17},{17,1},{2,18},{18,2},{3,19},{19,3},{4,20},{20... | collective-permute-start | bytes 1376264 | tf_op jit(solution)/shard_map/ppermute | solution.py:353
  74.9 0.5 collective-permute-start.18
  75.4 3.0 %collective-permute-done.9.refs_11_.refs_8_ = bf16[512,384]{1,0:T(8,128)(2,1)S(1)} collective-permute-done((bf16[512,384]{1,0:T(8,128)(2,1)}, bf16[512,384]{1,0:T(8,128)(2,1)S(1)}, u32[]{:S(2)}, u32[]{:S(2)}) %collective-permute-start.9) | collective-permute-done | bytes 393248 | tf_op jit(solution)/shard_map/ppermute | solution.py:361
  78.4 1.5 %collective-permute-start.20 = (bf16[256,896]{1,0:T(8,128)(2,1)}, bf16[256,896]{1,0:T(8,128)(2,1)}, u32[]{:S(2)}, u32[]{:S(2)}) collective-permute-start(bf16[256,896]{1,0:T(8,128)(2,1)} %collective-permute-done.19.refs_6_), channel_id=1, source_target_pairs={{0,16},{16,0},{1,17},{17,1},{2,18},{18,2},{3,19},{19,3},{4,20},{20... | collective-permute-start | bytes 1376264 | tf_op jit(solution)/shard_map/ppermute | solution.py:353
  79.9 5.1 %collective-permute-done.10.refs_12_.refs_9_.refs_10_ = bf16[512,384]{1,0:T(8,128)(2,1)S(1)} collective-permute-done((bf16[512,384]{1,0:T(8,128)(2,1)}, bf16[512,384]{1,0:T(8,128)(2,1)S(1)}, u32[]{:S(2)}, u32[]{:S(2)}) %collective-permute-start.10) | collective-permute-done | bytes 393248 | tf_op jit(solution)/shard_map/ppermute | solution.py:361
  85.0 0.6 collective-permute-start.12
  85.6 1.5 %collective-permute-start.13 = (bf16[512,384]{1,0:T(8,128)(2,1)S(1)}, bf16[512,384]{1,0:T(8,128)(2,1)S(1)}, u32[]{:S(2)}, u32[]{:S(2)}) collective-permute-start(bf16[512,384]{1,0:T(8,128)(2,1)S(1)} %collective-permute-done.11.refs_13_.refs_12_), channel_id=1, source_target_pairs={{0,2},{1,3},{2,0},{3,1},{4,6},{5,7},{6,4},{7,5},{8,10},{9,11},{10,... | collective-permute-start | bytes 1179656 | tf_op jit(solution)/shard_map/ppermute | solution.py:361
  87.1 0.6 pad_add_fusion.1.place_ref
  87.7 0.7 pad_add_fusion.place_ref
  88.4 8.1 %shard_map.85 = (f32[512,896]{1,0:T(8,128)}, f32[512,896]{1,0:T(8,128)}) custom-call(s32[4]{0:T(128)} %pad_add_fusion.1.place_ref, bf16[1024,4096]{1,0:T(8,128)(2,1)} %get-tuple-element.16.refs_0_.refs_1_.refs_2_.refs_3_.refs_4_.refs_5_.refs_6_.refs_7_, ...), custom_call_target="tpu_custom_call", output_to_operand_aliasing={{0}: (11, {}), {1}: (12, {})} | custom-call | flops 1879048192 | bytes 11272192 | tf_op jit(solution)/shard_map/pallas_call | solution.py:242
  96.4 0.0 copy-start.20
  96.5 0.5 collective-permute-done.13.refs_15_.refs_14_
  97.0 0.2 copy-done.20
  97.2 0.2 copy-done.21
  97.4 0.1 copy-done.14
  97.5 0.2 copy-done.15
  97.7 8.1 %shard_map.86 = (f32[512,896]{1,0:T(8,128)}, f32[512,896]{1,0:T(8,128)}) custom-call(s32[4]{0:T(128)} %pad_add_fusion.place_ref, bf16[1024,4096]{1,0:T(8,128)(2,1)} %get-tuple-element.16.refs_0_.refs_1_.refs_2_.refs_3_.refs_4_.refs_5_.refs_6_.refs_7_, ...), custom_call_target="tpu_custom_call", output_to_operand_aliasing={{0}: (16, {}), {1}: (17, {})} | custom-call | flops 1879048192 | bytes 11272192 | tf_op jit(solution)/shard_map/pallas_call | solution.py:242
  105.8 0.7 stack.87.place_ref
  106.5 0.0 copy-start.4
  106.5 0.0 copy-start.6
  106.5 0.0 copy-start.7
  106.5 10.4 %shard_map.84 = (f32[512,384]{1,0:T(8,128)}, f32[512,384]{1,0:T(8,128)}) custom-call(s32[8]{0:T(128)} %stack.87.place_ref, bf16[1024,4096]{1,0:T(8,128)(2,1)} %get-tuple-element.16.refs_0_.refs_1_.refs_2_.refs_3_.refs_4_.refs_5_.refs_6_.refs_7_, bf16[1024,4096]{1,0:T(8,128)(2,1)} %get-tuple-element.16.refs_0_.refs_1_.refs_2_.refs_3_.refs_4_.refs_5_.refs_6_.refs_7_, ...), custom_call_target="tpu_custom_call" | custom-call | flops 3221225472 | bytes 13107200 | tf_op jit(solution)/shard_map/pallas_call | solution.py:242
  116.9 0.6 collective-permute-start.14
  117.5 2.1 %collective-permute-done.14.got_b = f32[512,384]{1,0:T(8,128)S(1)} collective-permute-done((f32[512,384]{1,0:T(8,128)}, f32[512,384]{1,0:T(8,128)S(1)}, u32[]{:S(2)}, u32[]{:S(2)}) %collective-permute-start.14) | collective-permute-done | bytes 786464 | tf_op jit(solution)/shard_map/ppermute | solution.py:361
  119.6 0.0 copy-start.5
  119.7 1.1 copy-done.5
  120.8 15.1 %shard_map.87 = bf16[512,1024]{1,0:T(8,128)(2,1)} custom-call(s32[2]{0:T(128)S(1)} %copy-done.6, s32[2]{0:T(128)S(1)} %copy-done.7, f32[512,384]{1,0:T(8,128)S(1)} %copy-done.5, f32[512,384]{1,0:T(8,128)S(1)} %collective-permute-done.14.got_b, f32[512,896]{1,0:T(8,128)S(1)} %copy-done, f32[512,896]{1,0:T(8,128)} %collective-permute-done.23.got_a, ...), custom_call_target="tpu_custom_call" | custom-call | flops 2684354560 | bytes 20971520 | tf_op jit(solution)/shard_map/pallas_call | solution.py:312
  (55 shorter events, 0.2 us)
Async XLA Ops:
  0.0 21.9 %collective-permute-start = (bf16[512,8192]{1,0:T(8,128)(2,1)}, bf16[512,8192]{1,0:T(8,128)(2,1)}, u32[]{:S(2)}, u32[]{:S(2)}) collective-permute-start(bf16[512,8192]{1,0:T(8,128)(2,1)} %x_ref.1), channel_id=1, source_target_pairs={{0,1},{1,0},{2,3},{3,2},{4,5},{5,4},{6,7},{7,6},{8,9},{9,8},{10,11... | collective-permute-start | bytes 25165832 | tf_op jit(solution)/shard_map/ppermute | solution.py:361
  1.5 16.2 %collective-permute-start.4 = (bf16[256,896]{1,0:T(8,128)(2,1)S(1)}, bf16[256,896]{1,0:T(8,128)(2,1)}, u32[]{:S(2)}, u32[]{:S(2)}) collective-permute-start(bf16[256,896]{1,0:T(8,128)(2,1)S(1)} %constant_dynamic-slice_fusion), channel_id=1, source_target_pairs={{0,4},{1,5},{2,6},{3,7},{4,8},{5,9},{6,10},{7,11},{8,12},{9,13},{1... | collective-permute-start | bytes 1376264 | tf_op jit(solution)/shard_map/ppermute | solution.py:361
  4.1 34.2 %collective-permute-start.8 = (bf16[256,896]{1,0:T(8,128)(2,1)S(1)}, bf16[256,896]{1,0:T(8,128)(2,1)S(1)}, u32[]{:S(2)}, u32[]{:S(2)}) collective-permute-start(bf16[256,896]{1,0:T(8,128)(2,1)S(1)} %constant_dynamic-slice_fusion), channel_id=1, source_target_pairs={{0,12},{1,13},{2,14},{3,15},{4,0},{5,1},{6,2},{7,3},{8,4},{9,5},{1... | collective-permute-start | bytes 1376264 | tf_op jit(solution)/shard_map/ppermute | solution.py:361
  6.2 15.7 %collective-permute-start.3 = (bf16[256,896]{1,0:T(8,128)(2,1)S(1)}, bf16[256,896]{1,0:T(8,128)(2,1)}, u32[]{:S(2)}, u32[]{:S(2)}) collective-permute-start(bf16[256,896]{1,0:T(8,128)(2,1)S(1)} %constant_dynamic-slice_fusion), channel_id=1, source_target_pairs={{0,2},{1,3},{2,0},{3,1},{4,6},{5,7},{6,4},{7,5},{8,10},{9,11},{10,... | collective-permute-start | bytes 1376264 | tf_op jit(solution)/shard_map/ppermute | solution.py:361
  11.3 12.2 %copy-start.12 = (bf16[512,1280]{1,0:T(8,128)(2,1)S(1)}, bf16[512,1280]{1,0:T(8,128)(2,1)}, u32[]{:S(2)}) copy-start(bf16[512,1280]{1,0:T(8,128)(2,1)} %param.14) | copy-start | bytes 3932164
  17.7 31.0 %collective-permute-start.5 = (bf16[256,896]{1,0:T(8,128)(2,1)}, bf16[256,896]{1,0:T(8,128)(2,1)}, u32[]{:S(2)}, u32[]{:S(2)}) collective-permute-start(bf16[256,896]{1,0:T(8,128)(2,1)} %collective-permute-done.4.refs_9_), channel_id=1, source_target_pairs={{0,2},{1,3},{2,0},{3,1},{4,6},{5,7},{6,4},{7,5},{8,10},{9,11},{10,... | collective-permute-start | bytes 1376264 | tf_op jit(solution)/shard_map/ppermute | solution.py:361
  20.3 28.9 %collective-permute-start.7 = (bf16[256,896]{1,0:T(8,128)(2,1)}, bf16[256,896]{1,0:T(8,128)(2,1)}, u32[]{:S(2)}, u32[]{:S(2)}) collective-permute-start(bf16[256,896]{1,0:T(8,128)(2,1)} %collective-permute-done.4.refs_9_), channel_id=1, source_target_pairs={{0,16},{16,0},{1,17},{17,1},{2,18},{18,2},{3,19},{19,3},{4,20},{20... | collective-permute-start | bytes 1376264 | tf_op jit(solution)/shard_map/ppermute | solution.py:353
  21.9 32.0 %collective-permute-start.15 = (bf16[256,896]{1,0:T(8,128)(2,1)}, bf16[256,896]{1,0:T(8,128)(2,1)S(1)}, u32[]{:S(2)}, u32[]{:S(2)}) collective-permute-start(bf16[256,896]{1,0:T(8,128)(2,1)} %collective-permute-done.4.refs_9_), channel_id=1, source_target_pairs={{0,4},{1,5},{2,6},{3,7},{4,8},{5,9},{6,10},{7,11},{8,12},{9,13},{1... | collective-permute-start | bytes 1376264 | tf_op jit(solution)/shard_map/ppermute | solution.py:361
  21.9 28.8 %collective-permute-start.6 = (bf16[256,896]{1,0:T(8,128)(2,1)}, bf16[256,896]{1,0:T(8,128)(2,1)}, u32[]{:S(2)}, u32[]{:S(2)}) collective-permute-start(bf16[256,896]{1,0:T(8,128)(2,1)} %collective-permute-done.3.refs_8_), channel_id=1, source_target_pairs={{0,16},{16,0},{1,17},{17,1},{2,18},{18,2},{3,19},{19,3},{4,20},{20... | collective-permute-start | bytes 1376264 | tf_op jit(solution)/shard_map/ppermute | solution.py:353
  38.3 20.5 %copy-start.18 = (bf16[256,896]{1,0:T(8,128)(2,1)}, bf16[256,896]{1,0:T(8,128)(2,1)S(1)}, u32[]{:S(2)}) copy-start(bf16[256,896]{1,0:T(8,128)(2,1)S(1)} %collective-permute-done.8.refs_13_) | copy-start | bytes 1376260
  38.3 17.0 %collective-permute-start.1 = (bf16[512,384]{1,0:T(8,128)(2,1)}, bf16[512,384]{1,0:T(8,128)(2,1)S(1)}, u32[]{:S(2)}, u32[]{:S(2)}) collective-permute-start(bf16[512,384]{1,0:T(8,128)(2,1)} %get-tuple-element.17), channel_id=1, source_target_pairs={{0,4},{1,5},{2,6},{3,7},{4,8},{5,9},{6,10},{7,11},{8,12},{9,13},{1... | collective-permute-start | bytes 1179656 | tf_op jit(solution)/shard_map/ppermute | solution.py:361
  48.7 10.1 %collective-permute-start.2 = (bf16[512,384]{1,0:T(8,128)(2,1)}, bf16[512,384]{1,0:T(8,128)(2,1)S(1)}, u32[]{:S(2)}, u32[]{:S(2)}) collective-permute-start(bf16[512,384]{1,0:T(8,128)(2,1)} %get-tuple-element.17), channel_id=1, source_target_pairs={{0,2},{1,3},{2,0},{3,1},{4,6},{5,7},{6,4},{7,5},{8,10},{9,11},{10,... | collective-permute-start | bytes 1179656 | tf_op jit(solution)/shard_map/ppermute | solution.py:361
  49.3 23.5 %collective-permute-start.17 = (bf16[256,896]{1,0:T(8,128)(2,1)S(1)}, bf16[256,896]{1,0:T(8,128)(2,1)S(1)}, u32[]{:S(2)}, u32[]{:S(2)}) collective-permute-start(bf16[256,896]{1,0:T(8,128)(2,1)S(1)} %collective-permute-done.8.refs_13_), channel_id=1, source_target_pairs={{0,2},{1,3},{2,0},{3,1},{4,6},{5,7},{6,4},{7,5},{8,10},{9,11},{10,... | collective-permute-start | bytes 1376264 | tf_op jit(solution)/shard_map/ppermute | solution.py:361
  50.8 22.5 %collective-permute-start.21 = (bf16[256,896]{1,0:T(8,128)(2,1)S(1)}, bf16[256,896]{1,0:T(8,128)(2,1)}, u32[]{:S(2)}, u32[]{:S(2)}) collective-permute-start(bf16[256,896]{1,0:T(8,128)(2,1)S(1)} %collective-permute-done.8.refs_13_), channel_id=1, source_target_pairs={{0,16},{16,0},{1,17},{17,1},{2,18},{18,2},{3,19},{19,3},{4,20},{20... | collective-permute-start | bytes 1376264 | tf_op jit(solution)/shard_map/ppermute | solution.py:353
  53.9 19.4 %copy-start.16 = (bf16[256,896]{1,0:T(8,128)(2,1)}, bf16[256,896]{1,0:T(8,128)(2,1)S(1)}, u32[]{:S(2)}) copy-start(bf16[256,896]{1,0:T(8,128)(2,1)S(1)} %collective-permute-done.15.refs_4_) | copy-start | bytes 1376260
  53.9 19.4 %collective-permute-start.22 = (bf16[256,896]{1,0:T(8,128)(2,1)}, bf16[256,896]{1,0:T(8,128)(2,1)S(1)}, u32[]{:S(2)}, u32[]{:S(2)}) collective-permute-start(bf16[256,896]{1,0:T(8,128)(2,1)} %collective-permute-done.5.refs_10_), channel_id=1, source_target_pairs={{0,16},{16,0},{1,17},{17,1},{2,18},{18,2},{3,19},{19,3},{4,20},{20... | collective-permute-start | bytes 1376264 | tf_op jit(solution)/shard_map/ppermute | solution.py:353
  55.3 3.4 %copy-start.8 = (bf16[512,384]{1,0:T(8,128)(2,1)}, bf16[512,384]{1,0:T(8,128)(2,1)S(1)}, u32[]{:S(2)}) copy-start(bf16[512,384]{1,0:T(8,128)(2,1)S(1)} %collective-permute-done.1.refs_14_.refs_9_.refs_8_) | copy-start | bytes 1179652
  55.3 19.5 %collective-permute-start.19 = (bf16[256,896]{1,0:T(8,128)(2,1)S(1)}, bf16[256,896]{1,0:T(8,128)(2,1)}, u32[]{:S(2)}, u32[]{:S(2)}) collective-permute-start(bf16[256,896]{1,0:T(8,128)(2,1)S(1)} %collective-permute-done.15.refs_4_), channel_id=1, source_target_pairs={{0,2},{1,3},{2,0},{3,1},{4,6},{5,7},{6,4},{7,5},{8,10},{9,11},{10,... | collective-permute-start | bytes 1376264 | tf_op jit(solution)/shard_map/ppermute | solution.py:361
  58.8 0.7 copy-start.9
  69.7 8.6 %collective-permute-start.9 = (bf16[512,384]{1,0:T(8,128)(2,1)}, bf16[512,384]{1,0:T(8,128)(2,1)S(1)}, u32[]{:S(2)}, u32[]{:S(2)}) collective-permute-start(bf16[512,384]{1,0:T(8,128)(2,1)} %get-tuple-element.18), channel_id=1, source_target_pairs={{0,12},{1,13},{2,14},{3,15},{4,0},{5,1},{6,2},{7,3},{8,4},{9,5},{1... | collective-permute-start | bytes 1179656 | tf_op jit(solution)/shard_map/ppermute | solution.py:361
  72.7 15.6 %copy-start.17 = (bf16[256,896]{1,0:T(8,128)(2,1)}, bf16[256,896]{1,0:T(8,128)(2,1)S(1)}, u32[]{:S(2)}) copy-start(bf16[256,896]{1,0:T(8,128)(2,1)S(1)} %collective-permute-done.17.refs_5_) | copy-start | bytes 1376260
  72.7 12.3 %collective-permute-start.10 = (bf16[512,384]{1,0:T(8,128)(2,1)}, bf16[512,384]{1,0:T(8,128)(2,1)S(1)}, u32[]{:S(2)}, u32[]{:S(2)}) collective-permute-start(bf16[512,384]{1,0:T(8,128)(2,1)} %copy-done.8), channel_id=1, source_target_pairs={{0,2},{1,3},{2,0},{3,1},{4,6},{5,7},{6,4},{7,5},{8,10},{9,11},{10,... | collective-permute-start | bytes 1179656 | tf_op jit(solution)/shard_map/ppermute | solution.py:361
  73.3 12.3 %collective-permute-start.11 = (bf16[512,384]{1,0:T(8,128)(2,1)}, bf16[512,384]{1,0:T(8,128)(2,1)S(1)}, u32[]{:S(2)}, u32[]{:S(2)}) collective-permute-start(bf16[512,384]{1,0:T(8,128)(2,1)} %copy-done.8), channel_id=1, source_target_pairs={{0,4},{1,5},{2,6},{3,7},{4,8},{5,9},{6,10},{7,11},{8,12},{9,13},{1... | collective-permute-start | bytes 1179656 | tf_op jit(solution)/shard_map/ppermute | solution.py:361
  73.3 12.2 %copy-start.19 = (bf16[256,896]{1,0:T(8,128)(2,1)}, bf16[256,896]{1,0:T(8,128)(2,1)S(1)}, u32[]{:S(2)}) copy-start(bf16[256,896]{1,0:T(8,128)(2,1)S(1)} %collective-permute-done.22.refs_7_) | copy-start | bytes 1376260
  73.3 23.1 %collective-permute-start.16 = (bf16[256,896]{1,0:T(8,128)(2,1)S(1)}, bf16[256,896]{1,0:T(8,128)(2,1)S(1)}, u32[]{:S(2)}, u32[]{:S(2)}) collective-permute-start(bf16[256,896]{1,0:T(8,128)(2,1)S(1)} %collective-permute-done.15.refs_4_), channel_id=1, source_target_pairs={{0,16},{16,0},{1,17},{17,1},{2,18},{18,2},{3,19},{19,3},{4,20},{20... | collective-permute-start | bytes 1376264 | tf_op jit(solution)/shard_map/ppermute | solution.py:353
  74.9 21.6 %collective-permute-start.18 = (bf16[256,896]{1,0:T(8,128)(2,1)S(1)}, bf16[256,896]{1,0:T(8,128)(2,1)S(1)}, u32[]{:S(2)}, u32[]{:S(2)}) collective-permute-start(bf16[256,896]{1,0:T(8,128)(2,1)S(1)} %collective-permute-done.17.refs_5_), channel_id=1, source_target_pairs={{0,16},{16,0},{1,17},{17,1},{2,18},{18,2},{3,19},{19,3},{4,20},{20... | collective-permute-start | bytes 1376264 | tf_op jit(solution)/shard_map/ppermute | solution.py:353
  78.4 10.0 %copy-start.10 = (bf16[512,384]{1,0:T(8,128)(2,1)}, bf16[512,384]{1,0:T(8,128)(2,1)S(1)}, u32[]{:S(2)}) copy-start(bf16[512,384]{1,0:T(8,128)(2,1)S(1)} %collective-permute-done.9.refs_11_.refs_8_) | copy-start | bytes 1179652
  78.4 18.1 %collective-permute-start.20 = (bf16[256,896]{1,0:T(8,128)(2,1)}, bf16[256,896]{1,0:T(8,128)(2,1)}, u32[]{:S(2)}, u32[]{:S(2)}) collective-permute-start(bf16[256,896]{1,0:T(8,128)(2,1)} %collective-permute-done.19.refs_6_), channel_id=1, source_target_pairs={{0,16},{16,0},{1,17},{17,1},{2,18},{18,2},{3,19},{19,3},{4,20},{20... | collective-permute-start | bytes 1376264 | tf_op jit(solution)/shard_map/ppermute | solution.py:353
  85.0 3.4 %copy-start.11 = (bf16[512,384]{1,0:T(8,128)(2,1)}, bf16[512,384]{1,0:T(8,128)(2,1)S(1)}, u32[]{:S(2)}) copy-start(bf16[512,384]{1,0:T(8,128)(2,1)S(1)} %collective-permute-done.10.refs_12_.refs_9_.refs_10_) | copy-start | bytes 1179652
  85.0 11.5 %collective-permute-start.12 = (bf16[512,384]{1,0:T(8,128)(2,1)S(1)}, bf16[512,384]{1,0:T(8,128)(2,1)S(1)}, u32[]{:S(2)}, u32[]{:S(2)}) collective-permute-start(bf16[512,384]{1,0:T(8,128)(2,1)S(1)} %collective-permute-done.9.refs_11_.refs_8_), channel_id=1, source_target_pairs={{0,2},{1,3},{2,0},{3,1},{4,6},{5,7},{6,4},{7,5},{8,10},{9,11},{10,... | collective-permute-start | bytes 1179656 | tf_op jit(solution)/shard_map/ppermute | solution.py:361
  85.6 10.9 %copy-start.13 = (bf16[512,384]{1,0:T(8,128)(2,1)}, bf16[512,384]{1,0:T(8,128)(2,1)S(1)}, u32[]{:S(2)}) copy-start(bf16[512,384]{1,0:T(8,128)(2,1)S(1)} %collective-permute-done.11.refs_13_.refs_12_) | copy-start | bytes 1179652
  85.6 11.4 %collective-permute-start.13 = (bf16[512,384]{1,0:T(8,128)(2,1)S(1)}, bf16[512,384]{1,0:T(8,128)(2,1)S(1)}, u32[]{:S(2)}, u32[]{:S(2)}) collective-permute-start(bf16[512,384]{1,0:T(8,128)(2,1)S(1)} %collective-permute-done.11.refs_13_.refs_12_), channel_id=1, source_target_pairs={{0,2},{1,3},{2,0},{3,1},{4,6},{5,7},{6,4},{7,5},{8,10},{9,11},{10,... | collective-permute-start | bytes 1179656 | tf_op jit(solution)/shard_map/ppermute | solution.py:361
  96.4 0.8 copy-start.20
  96.5 0.9 copy-start.21
  96.5 1.0 copy-start.14
  97.0 0.7 copy-start.15
  105.8 13.8 %collective-permute-start.23 = (f32[512,896]{1,0:T(8,128)}, f32[512,896]{1,0:T(8,128)}, u32[]{:S(2)}, u32[]{:S(2)}) collective-permute-start(f32[512,896]{1,0:T(8,128)} %get-tuple-element.26), channel_id=1, source_target_pairs={{0,1},{1,0},{2,3},{3,2},{4,5},{5,4},{6,7},{7,6},{8,9},{9,8},{10,11... | collective-permute-start | bytes 5505032 | tf_op jit(solution)/shard_map/ppermute | solution.py:361
  106.5 11.0 %copy-start.22 = (f32[1280]{0:T(1024)S(1)}, f32[1280]{0:T(1024)}, u32[]{:S(2)}) copy-start(f32[1280]{0:T(1024)} %param.15) | copy-start | bytes 15364
  106.5 13.1 %copy-start = (f32[512,896]{1,0:T(8,128)S(1)}, f32[512,896]{1,0:T(8,128)}, u32[]{:S(2)}) copy-start(f32[512,896]{1,0:T(8,128)} %get-tuple-element.25.own_a) | copy-start | bytes 5505028
  106.5 13.1 %copy-start.1 = (f32[2,256,128]{2,1,0:T(8,128)S(1)}, f32[2,256,128]{2,1,0:T(8,128)}, u32[]{:S(2)}) copy-start(f32[2,256,128]{2,1,0:T(8,128)} %get-tuple-element.32.refs_1_.cos_ref) | copy-start | bytes 786436
  106.5 13.1 %copy-start.2 = (f32[2,256,128]{2,1,0:T(8,128)S(1)}, f32[2,256,128]{2,1,0:T(8,128)}, u32[]{:S(2)}) copy-start(f32[2,256,128]{2,1,0:T(8,128)} %get-tuple-element.33.refs_2_.sin_ref) | copy-start | bytes 786436
  106.5 13.1 %copy-start.3 = (f32[2,256,256]{2,1,0:T(8,128)S(1)}, f32[2,256,256]{2,1,0:T(8,128)}, u32[]{:S(2)}) copy-start(f32[2,256,256]{2,1,0:T(8,128)} %get-tuple-element.28.refs_0_.bias_ref) | copy-start | bytes 1572868
  106.5 13.1 %copy-start.4 = (bf16[2,2,1024,128]{3,2,1,0:T(8,128)(2,1)S(1)}, bf16[2,2,1024,128]{3,2,1,0:T(8,128)(2,1)}, u32[]{:S(2)}) copy-start(bf16[2,2,1024,128]{3,2,1,0:T(8,128)(2,1)} %cache_ref.1) | copy-start | bytes 3145732
  106.5 13.1 %copy-start.6 = (s32[2]{0:T(128)S(1)}, s32[2]{0:T(128)}, u32[]{:S(2)}) copy-start(s32[2]{0:T(128)} %kept_ref.1) | copy-start | bytes 28
  106.5 13.1 %copy-start.7 = (s32[2]{0:T(128)S(1)}, s32[2]{0:T(128)}, u32[]{:S(2)}) copy-start(s32[2]{0:T(128)} %len_ref.1) | copy-start | bytes 28
  116.9 2.7 %collective-permute-start.14 = (f32[512,384]{1,0:T(8,128)}, f32[512,384]{1,0:T(8,128)S(1)}, u32[]{:S(2)}, u32[]{:S(2)}) collective-permute-start(f32[512,384]{1,0:T(8,128)} %get-tuple-element.20), channel_id=1, source_target_pairs={{0,1},{1,0},{2,3},{3,2},{4,5},{5,4},{6,7},{7,6},{8,9},{9,8},{10,11... | collective-permute-start | bytes 2359304 | tf_op jit(solution)/shard_map/ppermute | solution.py:361
  119.6 1.1 copy-start.5
